TPU v7x, 32 devices: a whole 2x2x4 slice. The times are simulated.
32 devices in a mesh: parts: 2 (over x), cell: 16 (over z, y, core).
Axes of the slice: x: 2, y: 2, z: 4, core: 2. Of those that a mesh axis runs over, the one named last changes fastest.
Arguments:
- vectors: bfloat16 [49152, 768], P(('parts', 'cell')), parts along dimension 0, may hold values from -12 to 12
- row_slot: int32 [2, 49152], P(None, ('parts', 'cell')), parts along dimension 1, may hold values from 0 to 31, as said below
- fine_codes: int32 [2, 49152], P(None, ('parts', 'cell')), parts along dimension 1, may hold values from 0 to 2047
- cell_list: int32 [2, 1024], P(None, ('parts', 'cell')), parts along dimension 1, may hold values from 0 to 511, as said below
- coarse_in: float32 [8192, 768], P('cell'), may hold values from -6 to 6
- fine_in: float32 [2048, 768], replicated, may hold values from -6 to 6
Outputs:
- coarse_out: float32 [16384, 768], P(('parts', 'cell')), parts along dimension 0
- fine_out: float32 [4096, 768], P(('parts', 'cell')), parts along dimension 0
There are 2 independent parts, one for each index of `parts`. A program takes and returns all parts, laid end to end along the dimension named above; an argument that names none is the same for every part. Nothing has to cross between parts.
Inputs may be any that keep to these rules, and one draw needn't show every extreme that they name: In sweep 0, row_slot is nondecreasing over each device's 1536 vectors. `cell_list`: each run of 2 consecutive entries of a device's list is nondecreasing.
All inputs are finite; a program needn't handle non-finite values.
Results may differ from a plain program's by a relative error of at most 0.0028.
Values sent between devices are 32-bit elements; how exact they have to be, the bound alone decides.
No kernel may reach another device: no remote copies, remote signals or barrier semaphores. Data moves between devices by JAX's collectives and lax.ppermute only.
A program may use at most 128 MiB of HBM per device.

v0:
```python
import jax
import jax.numpy as jnp
from jax import lax
from jax.sharding import PartitionSpec as P


def code_tally(code_rows, codewords):
    return jax.ops.segment_sum(
        jnp.ones(code_rows.shape, jnp.float32), code_rows, num_segments=codewords
    )


def fine_update(code_term, totals_share, old_share, share_rows):
    part_sums = lax.psum_scatter(
        code_term(jnp.int32(0), lax.axis_size("cell") * share_rows),
        "cell",
        scatter_dimension=0,
        tiled=True,
    )
    return jnp.where(
        totals_share[:, None] > 0, part_sums / jnp.maximum(totals_share, 1.0)[:, None], old_share
    )


def per_device(vectors, row_slot, fine_codes, cell_list, coarse_in, fine_in):
    groups = lax.axis_size("cell")
    rows_here, feature = vectors.shape
    listed = cell_list.shape[1]
    slot_count = listed // groups
    owner_cells = coarse_in.shape[0]
    codewords = fine_in.shape[0]
    share_rows = codewords // groups
    share_start = lax.axis_index("cell") * share_rows
    fine_book = fine_in
    fine_share = lax.dynamic_slice_in_dim(fine_in, share_start, share_rows, 0)
    coarse = coarse_in
    list_iota = lax.iota(jnp.int32, listed)
    for sweep in range(2):
        code_totals = lax.psum(code_tally(fine_codes[sweep], codewords), "cell")
        slot_rows = row_slot[sweep]
        code_rows = fine_codes[sweep]
        picked = jnp.take(fine_book, code_rows, axis=0)
        residual = (vectors.astype(jnp.float32) - picked).astype(jnp.bfloat16)
        slot_hot = (slot_rows[None, :] == list_iota[:, None]).astype(jnp.bfloat16)
        slot_sums = jnp.dot(slot_hot, residual, preferred_element_type=jnp.float32)
        slot_counts = jnp.sum(slot_hot, axis=1, dtype=jnp.float32)
        slot_cells = cell_list[sweep].astype(jnp.float32)
        got_sums, got_counts, got_cells = (
            lax.all_to_all(
                slot_sums.reshape(groups, slot_count, feature),
                "cell",
                split_axis=0,
                concat_axis=0,
                tiled=True,
            ),
            lax.all_to_all(
                slot_counts.reshape(groups, slot_count),
                "cell",
                split_axis=0,
                concat_axis=0,
                tiled=True,
            ),
            lax.all_to_all(
                slot_cells.reshape(groups, slot_count),
                "cell",
                split_axis=0,
                concat_axis=0,
                tiled=True,
            ),
        )
        flat_cells = got_cells.reshape(groups * slot_count).astype(jnp.int32)
        cell_sums = jax.ops.segment_sum(
            got_sums.reshape(groups * slot_count, feature), flat_cells, num_segments=owner_cells
        )
        cell_counts = jax.ops.segment_sum(
            got_counts.reshape(groups * slot_count), flat_cells, num_segments=owner_cells
        )
        coarse = jnp.where(
            cell_counts[:, None] > 0, cell_sums / jnp.maximum(cell_counts, 1.0)[:, None], coarse
        )
        returned_rows = jnp.take(coarse, flat_cells, axis=0).reshape(groups, slot_count, feature)
        arrived = lax.all_to_all(returned_rows, "cell", split_axis=0, concat_axis=0, tiled=True)
        entry_centers = arrived.reshape(listed, feature)
        row_centers = jnp.take(entry_centers, slot_rows, axis=0)
        fine_residual = (vectors.astype(jnp.float32) - row_centers).astype(jnp.bfloat16)

        def code_term(start, count, code_rows=code_rows, fine_residual=fine_residual):
            wanted = start + lax.iota(jnp.int32, count)
            code_hot = (code_rows[None, :] == wanted[:, None]).astype(jnp.bfloat16)
            return jnp.dot(code_hot, fine_residual, preferred_element_type=jnp.float32)

        totals_share = lax.dynamic_slice_in_dim(code_totals, share_start, share_rows, 0)
        if sweep == 0:
            full_sums = lax.psum(code_term(0, codewords), "cell")
            fine_book = jnp.where(
                code_totals[:, None] > 0,
                full_sums / jnp.maximum(code_totals, 1.0)[:, None],
                fine_book,
            )
            fine_share = lax.dynamic_slice_in_dim(fine_book, share_start, share_rows, 0)
        else:
            fine_share = fine_update(code_term, totals_share, fine_share, share_rows)
    return (coarse, fine_share)


def solution(mesh):
    return jax.shard_map(
        per_device,
        mesh=mesh,
        in_specs=(
            P(("parts", "cell"), None),
            P(None, ("parts", "cell")),
            P(None, ("parts", "cell")),
            P(None, ("parts", "cell")),
            P("cell", None),
            P(),
        ),
        out_specs=(P(("parts", "cell"), None), P(("parts", "cell"), None)),
        check_vma=False,
    )
```

profile of v0, /device:TPU:0, one launch (start us, length us, event | category | flops | bytes accessed | tf_op | source)
XLA Modules:
  0.0 382.8 jit_solution(16782122988796526770)
XLA Ops:
  8.6 7.4 %all-to-all-start.2 = ((f32[16,1,2]{2,1,0:T(1,128)}), f32[16,1,2]{2,1,0:T(1,128)S(1)}, u32[]{:S(2)}, u32[]{:S(2)}) async-start(f32[16,1,2]{2,1,0:T(1,128)} %bitcast.2), calls=%async_computation.2 | async-start | bytes 16384 | tf_op jit(solution)/shard_map/all_to_all | solution.py:63
  17.9 9.7 %gather_fusion = f32[1536,768]{1,0:T(8,128)} fusion(f32[2048,768]{1,0:T(8,128)} %param.17, s32[2048]{0:T(1024)S(1)} %pad_clamp_fusion.3), kind=kCustom, calls=%fused_computation.clone | custom fusion | bytes 9443328 | tf_op jit(solution)/shard_map/jit(_take)/gather | solution.py:42
  27.5 3.2 fusion.12
  32.1 6.0 %all-to-all-start.3 = ((f32[16,1,2]{2,1,0:T(1,128)}), f32[16,1,2]{2,1,0:T(1,128)S(1)}, u32[]{:S(2)}, u32[]{:S(2)}) async-start(f32[16,1,2]{2,1,0:T(1,128)} %bitcast.3), calls=%async_computation.3 | async-start | bytes 16384 | tf_op jit(solution)/shard_map/all_to_all | solution.py:56
  38.3 6.3 %all-to-all-done.3 = f32[16,1,2]{2,1,0:T(1,128)S(1)} async-done(((f32[16,1,2]{2,1,0:T(1,128)}), f32[16,1,2]{2,1,0:T(1,128)S(1)}, u32[]{:S(2)}, u32[]{:S(2)}) %all-to-all-start.3) | async-done | bytes 160 | tf_op jit(solution)/shard_map/all_to_all | solution.py:56
  44.6 3.5 all-to-all-start.4
  50.2 5.3 %all-to-all-done.4 = f32[16,2,768]{2,1,0:T(2,128)S(1)} async-done(((f32[16,2,768]{2,1,0:T(2,128)}), f32[16,2,768]{2,1,0:T(2,128)S(1)}, u32[]{:S(2)}, u32[]{:S(2)}) %all-to-all-start.4) | async-done | bytes 98336 | tf_op jit(solution)/shard_map/all_to_all | solution.py:49
  56.7 1.6 divide_select_fusion.2
  59.7 3.5 all-to-all-start.5
  63.3 7.3 %all-to-all-done.5 = f32[16,2,768]{2,1,0:T(2,128)S(1)} async-done(((f32[16,2,768]{2,1,0:T(2,128)}), f32[16,2,768]{2,1,0:T(2,128)S(1)}, u32[]{:S(2)}, u32[]{:S(2)}) %all-to-all-start.5) | async-done | bytes 98336 | tf_op jit(solution)/shard_map/all_to_all | solution.py:82
  70.7 5.6 %gather_fusion.2 = f32[1536,768]{1,0:T(8,128)} fusion(f32[32,768]{1,0:T(8,128)S(1)} %reshape.136, s32[2048]{0:T(1024)S(1)} %pad_clamp_fusion.2), kind=kCustom, calls=%fused_computation.2.clone | custom fusion | bytes 9443328 | tf_op jit(solution)/shard_map/jit(_take)/gather | solution.py:84
  76.3 11.1 %fusion = f32[2048,768]{1,0:T(8,128)} fusion(s32[1536]{0:T(1024)S(1)} %get-tuple-element.8, bf16[1536,768]{1,0:T(8,128)(2,1)} %param.12, f32[1536,768]{1,0:T(8,128)} %gather_fusion.2, pred[1536]{0:T(1024)(128)(4,1)S(1)} %compare_and_fusion.2), kind=kOutput, calls=%fused_computation.14 | convolution fusion | flops 4839702528 | bytes 13377024 | tf_op jit(solution)/shard_map/dot_general | solution.py:90
  88.2 3.5 all-to-all-start
  91.7 8.7 %scatter_custom_fusion.1 = f32[2048]{0:T(1024)S(1)} fusion(s32[1536]{0:T(1024)S(1)} %get-tuple-element.8, f32[1536]{0:T(1024)S(1)} %broadcast.42, f32[]{:T(128)} %constant.30.clone.1), kind=kCustom, calls=%fused_computation.78 | custom fusion | flops 1536 | bytes 8196 | tf_op jit(solution)/shard_map/scatter-add | solution.py:8
  100.3 8.7 %scatter_custom_fusion.5 = f32[2048]{0:T(1024)S(1)} fusion(s32[1536]{0:T(1024)S(1)} %get-tuple-element.7, f32[1536]{0:T(1024)S(1)} %broadcast.42, f32[]{:T(128)} %constant.30.clone.1), kind=kCustom, calls=%fused_computation.75 | custom fusion | flops 1536 | bytes 8196 | tf_op jit(solution)/shard_map/scatter-add | solution.py:8
  109.0 63.3 %all-reduce = (f32[2048]{0:T(1024)S(1)}, f32[2048]{0:T(1024)S(1)}) all-reduce(f32[2048]{0:T(1024)S(1)} %scatter_custom_fusion.1, f32[2048]{0:T(1024)S(1)} %scatter_custom_fusion.5), channel_id=1, replica_groups=mesh['parts'=2,'cell'=16] {'cell'}, use_global_device_ids=true, to_apply=%region_3.4 | all-reduce | flops 4096 | bytes 32768 | tf_op jit(solution)/shard_map/psum | solution.py:39
  173.2 3.7 all-to-all-start.1
  177.0 6.0 %all-to-all-done.1 = f32[16,1,2]{2,1,0:T(1,128)S(1)} async-done(((f32[16,1,2]{2,1,0:T(1,128)}), f32[16,1,2]{2,1,0:T(1,128)S(1)}, u32[]{:S(2)}, u32[]{:S(2)}) %all-to-all-start.1) | async-done | bytes 160 | tf_op jit(solution)/shard_map/all_to_all | solution.py:56
  184.5 40.1 %all-reduce.3.cloned.1.call-done = f32[2048,768]{1,0:T(8,128)} async-done(((f32[2048,768]{1,0:T(8,128)}), f32[2048,768]{1,0:T(8,128)}) %all-reduce.3.cloned.1.call-update) | async-done | bytes 6291472 | tf_op jit(solution)/shard_map/psum | solution.py:94
  224.6 7.7 %divide_select_fusion = f32[2048,768]{1,0:T(8,128)} fusion(f32[2048,768]{1,0:T(8,128)} %param.17, f32[2048,768]{1,0:T(8,128)} %all-reduce.3.cloned.1.call-done, f32[2048]{0:T(1024)S(1)} %broadcast_maximum_fusion, pred[2048]{0:T(1024)(128)(4,1)S(1)} %broadcast_compare_fusion), kind=kLoop, calls=%fused_computation.21 | loop fusion | flops 3145728 | bytes 18884608 | tf_op jit(solution)/shard_map/jit(_where)/select_n | solution.py:95
  232.4 9.6 %gather_fusion.3 = f32[1536,768]{1,0:T(8,128)} fusion(f32[2048,768]{1,0:T(8,128)} %divide_select_fusion, s32[2048]{0:T(1024)S(1)} %pad_clamp_fusion.1), kind=kCustom, calls=%fused_computation.3.clone | custom fusion | bytes 9443328 | tf_op jit(solution)/shard_map/jit(_take)/gather | solution.py:42
  242.0 3.9 %fusion.9 = f32[32,768]{1,0:T(8,128)S(1)} fusion(bf16[1536,768]{1,0:T(8,128)(2,1)} %param.12, f32[1536,768]{1,0:T(8,128)} %gather_fusion.3, pred[1536]{0:T(1024)(128)(4,1)S(1)} %compare_and_fusion.1, s32[1536]{0:T(1024)S(1)} %get-tuple-element.4), kind=kOutput, calls=%fused_computation.27 | convolution fusion | flops 80265216 | bytes 7183872 | tf_op jit(solution)/shard_map/dot_general | solution.py:45
  246.6 4.8 %all-to-all-start.6 = ((f32[16,2,768]{2,1,0:T(2,128)}), f32[16,2,768]{2,1,0:T(2,128)S(1)}, u32[]{:S(2)}, u32[]{:S(2)}) async-start(f32[16,2,768]{2,1,0:T(2,128)} %reshape.137), calls=%async_computation.6 | async-start | bytes 196608 | tf_op jit(solution)/shard_map/all_to_all | solution.py:49
  251.4 7.4 %all-to-all-done.6 = f32[16,2,768]{2,1,0:T(2,128)S(1)} async-done(((f32[16,2,768]{2,1,0:T(2,128)}), f32[16,2,768]{2,1,0:T(2,128)S(1)}, u32[]{:S(2)}, u32[]{:S(2)}) %all-to-all-start.6) | async-done | bytes 98336 | tf_op jit(solution)/shard_map/all_to_all | solution.py:49
  260.0 1.4 divide_select_fusion.1
  261.4 2.1 gather_fusion.4
  264.2 3.5 all-to-all-start.7
  267.8 7.3 %all-to-all-done.7 = f32[16,2,768]{2,1,0:T(2,128)S(1)} async-done(((f32[16,2,768]{2,1,0:T(2,128)}), f32[16,2,768]{2,1,0:T(2,128)S(1)}, u32[]{:S(2)}, u32[]{:S(2)}) %all-to-all-start.7) | async-done | bytes 98336 | tf_op jit(solution)/shard_map/all_to_all | solution.py:82
  275.2 5.6 %gather_fusion.5 = f32[1536,768]{1,0:T(8,128)} fusion(f32[32,768]{1,0:T(8,128)S(1)} %reshape.140, s32[2048]{0:T(1024)S(1)} %pad_clamp_fusion), kind=kCustom, calls=%fused_computation.5.clone | custom fusion | bytes 9443328 | tf_op jit(solution)/shard_map/jit(_take)/gather | solution.py:84
  280.8 10.4 %fusion.1 = f32[2048,768]{1,0:T(8,128)} fusion(s32[1536]{0:T(1024)S(1)} %get-tuple-element.7, bf16[1536,768]{1,0:T(8,128)(2,1)S(1)} %copy-done.1, f32[1536,768]{1,0:T(8,128)} %gather_fusion.5, pred[1536]{0:T(1024)(128)(4,1)S(1)} %compare_and_fusion), kind=kOutput, calls=%fused_computation.15 | convolution fusion | flops 4839702528 | bytes 13377024 | tf_op jit(solution)/shard_map/dot_general | solution.py:90
  291.3 82.6 %reduce-scatter.2.cloned.1.call-done = f32[128,768]{1,0:T(8,128)} async-done(((f32[2048,768]{1,0:T(8,128)}), f32[128,768]{1,0:T(8,128)}) %reduce-scatter.2.cloned.1.call-update) | async-done | bytes 393232 | tf_op jit(solution)/shard_map/reduce_scatter | solution.py:14
  374.0 2.0 dynamic-slice_select_fusion
  (70 shorter events, 15.8 us)
Async XLA Ops:
  8.6 23.5 %all-to-all-start.2 = ((f32[16,1,2]{2,1,0:T(1,128)}), f32[16,1,2]{2,1,0:T(1,128)S(1)}, u32[]{:S(2)}, u32[]{:S(2)}) async-start(f32[16,1,2]{2,1,0:T(1,128)} %bitcast.2), calls=%async_computation.2 | async-start | bytes 16384 | tf_op jit(solution)/shard_map/all_to_all | solution.py:63
  17.8 9.7 %copy-start = (bf16[1536,768]{1,0:T(8,128)(2,1)S(1)}, bf16[1536,768]{1,0:T(8,128)(2,1)}, u32[]{:S(2)}) copy-start(bf16[1536,768]{1,0:T(8,128)(2,1)} %param.12) | copy-start | bytes 7077892
  32.1 12.4 %all-to-all-start.3 = ((f32[16,1,2]{2,1,0:T(1,128)}), f32[16,1,2]{2,1,0:T(1,128)S(1)}, u32[]{:S(2)}, u32[]{:S(2)}) async-start(f32[16,1,2]{2,1,0:T(1,128)} %bitcast.3), calls=%async_computation.3 | async-start | bytes 16384 | tf_op jit(solution)/shard_map/all_to_all | solution.py:56
  44.6 10.9 %all-to-all-start.4 = ((f32[16,2,768]{2,1,0:T(2,128)}), f32[16,2,768]{2,1,0:T(2,128)S(1)}, u32[]{:S(2)}, u32[]{:S(2)}) async-start(f32[16,2,768]{2,1,0:T(2,128)} %reshape.133), calls=%async_computation.4 | async-start | bytes 196608 | tf_op jit(solution)/shard_map/all_to_all | solution.py:49
  59.7 10.9 %all-to-all-start.5 = ((f32[16,2,768]{2,1,0:T(2,128)}), f32[16,2,768]{2,1,0:T(2,128)S(1)}, u32[]{:S(2)}, u32[]{:S(2)}) async-start(f32[16,2,768]{2,1,0:T(2,128)} %reshape.135), calls=%async_computation.5 | async-start | bytes 196608 | tf_op jit(solution)/shard_map/all_to_all | solution.py:82
  63.3 161.4 %all-reduce.3.cloned.1.call-start = ((), (), s32[]{:S(2)}) async-start(), calls=%async_computation.9 | async-start | bytes 12582912 | tf_op jit(solution)/shard_map/psum | solution.py:94
  88.2 85.0 %all-to-all-start = ((f32[16,1,2]{2,1,0:T(1,128)}), f32[16,1,2]{2,1,0:T(1,128)S(1)}, u32[]{:S(2)}, u32[]{:S(2)}) async-start(f32[16,1,2]{2,1,0:T(1,128)} %bitcast), calls=%async_computation | async-start | bytes 16384 | tf_op jit(solution)/shard_map/all_to_all | solution.py:63
  173.2 9.8 %all-to-all-start.1 = ((f32[16,1,2]{2,1,0:T(1,128)}), f32[16,1,2]{2,1,0:T(1,128)S(1)}, u32[]{:S(2)}, u32[]{:S(2)}) async-start(f32[16,1,2]{2,1,0:T(1,128)} %bitcast.1), calls=%async_computation.1 | async-start | bytes 16384 | tf_op jit(solution)/shard_map/all_to_all | solution.py:56
  246.6 12.2 %all-to-all-start.6 = ((f32[16,2,768]{2,1,0:T(2,128)}), f32[16,2,768]{2,1,0:T(2,128)S(1)}, u32[]{:S(2)}, u32[]{:S(2)}) async-start(f32[16,2,768]{2,1,0:T(2,128)} %reshape.137), calls=%async_computation.6 | async-start | bytes 196608 | tf_op jit(solution)/shard_map/all_to_all | solution.py:49
  264.2 10.9 %all-to-all-start.7 = ((f32[16,2,768]{2,1,0:T(2,128)}), f32[16,2,768]{2,1,0:T(2,128)S(1)}, u32[]{:S(2)}, u32[]{:S(2)}) async-start(f32[16,2,768]{2,1,0:T(2,128)} %reshape.139), calls=%async_computation.7 | async-start | bytes 196608 | tf_op jit(solution)/shard_map/all_to_all | solution.py:82
  267.7 106.2 %reduce-scatter.2.cloned.1.call-start = ((), (), s32[]{:S(2)}) async-start(), calls=%async_computation.10 | async-start | bytes 6684672 | tf_op jit(solution)/shard_map/reduce_scatter | solution.py:14
  275.2 5.6 %copy-start.1 = (bf16[1536,768]{1,0:T(8,128)(2,1)S(1)}, bf16[1536,768]{1,0:T(8,128)(2,1)}, u32[]{:S(2)}) copy-start(bf16[1536,768]{1,0:T(8,128)(2,1)} %param.12) | copy-start | bytes 7077892
Sparse Core Ops, SparseCore 0:
  87.6 136.9 all-reduce.2
  291.3 82.6 reduce-scatter.1
where the time goes:
time: 384 us; the launch traced here: 383 us
  waiting for transfers between devices  162 us (42%)
  blocking collectives  63.3 us (16%)
  local copies, waits for them, and re-layouts  41.6 us (11%)
  other arithmetic  36.8 us (10%)
  starting transfers between devices  35.9 us (9%)
  matrix products  28.5 us (7%)
  between operations  14.4 us (4%)
    reduce_scatter x1, waiting for transfers between devices, fine_update(): lax.psum_scatter(code_term(jnp.int32(0), lax.axis_size('cell') * share_ro...  82.6 us
    psum x1, blocking collectives, per_device(): code_totals = lax.psum(code_tally(fine_codes[sweep], codewords), 'cell')  63.3 us
    psum x1, waiting for transfers between devices, per_device(): full_sums = lax.psum(code_term(0, codewords), 'cell')  40.1 us
    dot_general x2, matrix products, code_term(): return jnp.dot(code_hot, fine_residual, preferred_element_type=jnp.float32)  21.5 us
    gather x2, local copies, waits for them, and re-layouts, per_device(): picked = jnp.take(fine_book, code_rows, axis=0)  19.3 us
    scatter-add x2, other arithmetic, code_tally(): jax.ops.segment_sum(jnp.ones(code_rows.shape, jnp.float32), code_rows, nu...  17.3 us
    all_to_all x2, waiting for transfers between devices, per_device(): lax.all_to_all(returned_rows, 'cell', split_axis=0, concat_axis=0, tiled=...  14.6 us
    all_to_all x2, waiting for transfers between devices, per_device(): lax.all_to_all(slot_sums.reshape(groups, slot_count, feature), 'cell', sp...  12.7 us
  transfers between devices with their start and end apart: 10, of which 8 were waited for; matrix products, arithmetic and copies ran while one was open for 10% of the time, Pallas kernels for 0%

commit v1 on v0

--- a/solution.py
+++ b/solution.py
@@ -22,7 +22,7 @@
     )
 
 
-def per_device(vectors, row_slot, fine_codes, cell_list, coarse_in, fine_in):
+def routed_plan(vectors, row_slot, fine_codes, cell_list, coarse_in, fine_in):
     groups = lax.axis_size("cell")
     rows_here, feature = vectors.shape
     listed = cell_list.shape[1]
@@ -102,6 +102,140 @@
             fine_share = fine_update(code_term, totals_share, fine_share, share_rows)
     return (coarse, fine_share)
 
+HIGH = lax.Precision.HIGHEST
+
+
+def exact_dot(left, right):
+    return jnp.dot(left, right, precision=HIGH, preferred_element_type=jnp.float32)
+
+
+def hot(codes, count):
+    return (codes[..., None, :] == lax.iota(jnp.int32, count)[:, None]).astype(jnp.bfloat16)
+
+
+def pair_counts(codes, slots, codewords, listed):
+    groups = codes.shape[0]
+    low = 256
+    high = codewords // low
+    left = hot((codes // low) * listed + slots, high * listed)
+    right = hot(codes % low, low)
+    tables = lax.dot_general(
+        left, right, (((2,), (2,)), ((0,), (0,))), preferred_element_type=jnp.float32
+    )
+    tables = tables.reshape(groups, high, listed, low)
+    return tables.transpose(0, 2, 1, 3).reshape(groups * listed, codewords)
+
+
+def dense_plan(vectors, row_slot, fine_codes, cell_list, coarse_in, fine_in):
+    groups = lax.axis_size("cell")
+    me = lax.axis_index("cell")
+    rows_here, feature = vectors.shape
+    listed = cell_list.shape[1]
+    slot_count = listed // groups
+    owner_cells = coarse_in.shape[0]
+    codewords = fine_in.shape[0]
+    share_rows = codewords // groups
+    share_start = me * share_rows
+    entries = groups * listed
+
+    codes = jnp.concatenate([fine_codes, row_slot], axis=1)
+    codes = jnp.concatenate([codes, cell_list], axis=1)
+    gathered = lax.all_gather(codes.reshape(-1), "cell").reshape(groups, 2, -1)
+    all_fine = gathered[:, :, :rows_here]
+    all_slot = gathered[:, :, rows_here : 2 * rows_here]
+    all_cell = gathered[:, :, 2 * rows_here :]
+
+    own_hot = [hot(row_slot[t], listed) for t in range(2)]
+    code_hot = [hot(fine_codes[t], codewords) for t in range(2)]
+    own_sums = [
+        jnp.dot(own_hot[t], vectors, preferred_element_type=jnp.float32) for t in range(2)
+    ]
+    fine_sums = [
+        jnp.dot(code_hot[t], vectors, preferred_element_type=jnp.float32) for t in range(2)
+    ]
+    own_pairs = pair_counts(fine_codes[0][None], row_slot[0][None], codewords, listed)
+    first_sums = lax.all_gather(
+        own_sums[0] - exact_dot(own_pairs, fine_in), "cell", tiled=True
+    )
+
+    pairs = [
+        pair_counts(all_fine[:, t], all_slot[:, t], codewords, listed) for t in range(2)
+    ]
+    code_totals = [jnp.sum(pairs[t], axis=0) for t in range(2)]
+    entry_totals = [jnp.sum(pairs[t], axis=1) for t in range(2)]
+    owner_of = (lax.iota(jnp.int32, entries) % listed) // slot_count
+    cell_of = [
+        all_cell[:, t].reshape(entries) + owner_of * owner_cells for t in range(2)
+    ]
+    same = [(cell_of[t][:, None] == cell_of[t][None, :]).astype(jnp.float32) for t in range(2)]
+    cell_totals = [exact_dot(same[t], entry_totals[t][:, None]) for t in range(2)]
+
+    kept_sums = jnp.where(code_totals[1][:, None] > 0, fine_sums[1], fine_sums[0])
+    share_sums = lax.psum_scatter(kept_sums, "cell", scatter_dimension=0, tiled=True)
+
+    fine_here = jnp.where(
+        (lax.iota(jnp.int32, codewords) // share_rows == me) & (code_totals[0] == 0), 1.0, 0.0
+    )
+    fine_terms = jnp.where(fine_here[:, None] > 0, fine_in, fine_sums[0])
+    weights = pairs[1] / jnp.maximum(code_totals[0], 1.0)[None, :]
+    bracket = -exact_dot(weights, fine_terms)
+    bracket = bracket + jnp.where(
+        (lax.iota(jnp.int32, entries) // listed == me)[:, None],
+        jnp.tile(own_sums[1], (groups, 1)),
+        0.0,
+    )
+    bracket = bracket.reshape(groups, groups, slot_count, feature).transpose(1, 0, 2, 3)
+    bracket = lax.psum_scatter(
+        bracket.reshape(entries, feature), "cell", scatter_dimension=0, tiled=True
+    )
+
+    first_centers = exact_dot(same[0], first_sums) / jnp.maximum(cell_totals[0], 1.0)
+
+    def owned(table):
+        parts = table.reshape(groups, groups, slot_count, *table.shape[1:])
+        return lax.dynamic_index_in_dim(parts, me, 1, keepdims=False).reshape(
+            listed, *table.shape[1:]
+        )
+
+    mixing = exact_dot(owned(weights), pairs[0].T)
+    second_sums = bracket + exact_dot(mixing, first_centers)
+    own_cells = [owned(all_cell[:, t].reshape(entries)) for t in range(2)]
+    own_totals = [owned(entry_totals[t]) for t in range(2)]
+    own_same = (own_cells[1][:, None] == own_cells[1][None, :]).astype(jnp.float32)
+    own_centers = exact_dot(own_same, second_sums) / jnp.maximum(
+        exact_dot(own_same, own_totals[1][:, None]), 1.0
+    )
+    second_centers = lax.all_gather(own_centers, "cell")
+    second_centers = (
+        second_centers.reshape(groups, groups, slot_count, feature)
+        .transpose(1, 0, 2, 3)
+        .reshape(entries, feature)
+    )
+
+    coarse = coarse_in
+    for t, sums in enumerate((owned(first_sums), second_sums)):
+        picks = hot(own_cells[t], owner_cells).astype(jnp.float32)
+        counts = exact_dot(picks, own_totals[t][:, None])
+        coarse = jnp.where(counts > 0, exact_dot(picks, sums) / jnp.maximum(counts, 1.0), coarse)
+
+    def share(table, axis):
+        return lax.dynamic_slice_in_dim(table, share_start, share_rows, axis)
+
+    counts = [share(code_totals[t], 0)[:, None] for t in range(2)]
+    away = [
+        exact_dot(share(pairs[t], 1).T, centers)
+        for t, centers in enumerate((first_centers, second_centers))
+    ]
+    fine = jnp.where(counts[0] > 0, (share_sums - away[0]) / jnp.maximum(counts[0], 1.0), share(fine_in, 0))
+    fine = jnp.where(counts[1] > 0, (share_sums - away[1]) / jnp.maximum(counts[1], 1.0), fine)
+    return (coarse, fine)
+
+
+def per_device(vectors, row_slot, fine_codes, cell_list, coarse_in, fine_in):
+    entries = lax.axis_size("cell") * cell_list.shape[1]
+    plan = dense_plan if entries <= fine_in.shape[1] else routed_plan
+    return plan(vectors, row_slot, fine_codes, cell_list, coarse_in, fine_in)
+
 
 def solution(mesh):
     return jax.shard_map(

time: 384 us -> 314 us (0.82)
  matrix products: 28.5 us -> 75.5 us
  waiting for transfers between devices: 162 us -> 115 us
  blocking collectives: 63.3 us -> 24.7 us
  starting transfers between devices: 35.9 us -> 0.38 us
  local copies, waits for them, and re-layouts: 41.6 us -> 63 us
  other arithmetic: 36.8 us -> 16.3 us
    psum x1 -> x0, blocking collectives: 63.3 us -> none  [per_device(): code_totals = lax.psum(code_tally(fine_codes[sweep], codewords), 'cell')]
    dot_general x4 -> x21, matrix products: 28.5 us -> 75.5 us  [the longest x14 43.9 us: exact_dot(): jnp.dot(left, right, precision=HIGH, preferred_element_type=jnp.float32)]
    psum x1 -> x0, waiting for transfers between devices: 40.1 us -> none  [per_device(): full_sums = lax.psum(code_term(0, codewords), 'cell')]
    all_to_all x8 -> x0, waiting for transfers between devices: 39.6 us -> none  [the longest x2 14.6 us: per_device(): lax.all_to_all(returned_rows, 'cell', split_axis=0, concat_axis=0, tiled=...]
    all_to_all x8 -> x0, starting transfers between devices: 35.8 us -> none  [the longest x2 10.9 us: per_device(): lax.all_to_all(slot_cells.reshape(groups, slot_count), 'cell', split_axis...]
    gather x6 -> x0, local copies, waits for them, and re-layouts: 33.2 us -> none  [the longest x2 19.3 us: per_device(): picked = jnp.take(fine_book, code_rows, axis=0)]
    reshape x10 -> x11, local copies, waits for them, and re-layouts: 3.23 us -> 36.3 us  [the longest x2 12 us: pair_counts(): tables = tables.reshape(groups, high, listed, low)]
    all_gather x0 -> x1, blocking collectives: none -> 24.7 us  [dense_plan(): gathered = lax.all_gather(codes.reshape(-1), 'cell').reshape(groups, 2, -1)]
  transfers between devices with their start and end apart: 10 -> 4, of which waited for: 8 -> 3; matrix products, arithmetic and copies ran while one was open for 10% -> 43% of each run, Pallas kernels for 0% -> 0%
where the time goes in v1:
time: 314 us; the launch traced here: 309 us
  waiting for transfers between devices  115 us (37%)
  matrix products  75.5 us (24%)
  local copies, waits for them, and re-layouts  63 us (20%)
  blocking collectives  24.7 us (8%)
  other arithmetic  16.3 us (5%)
  between operations  14.4 us (5%)
    reduce_scatter x1, waiting for transfers between devices, dense_plan(): lax.psum_scatter(kept_sums, 'cell', scatter_dimension=0, tiled=True)  78.9 us
    dot_general x14, matrix products, exact_dot(): jnp.dot(left, right, precision=HIGH, preferred_element_type=jnp.float32)  43.9 us
    all_gather x1, blocking collectives, dense_plan(): gathered = lax.all_gather(codes.reshape(-1), 'cell').reshape(groups, 2, -1)  24.7 us
    all_gather x1, waiting for transfers between devices, dense_plan(): second_centers = lax.all_gather(own_centers, 'cell')  19.8 us
    reduce_scatter x1, waiting for transfers between devices, dense_plan(): lax.psum_scatter(bracket.reshape(entries, feature), 'cell', scatter_dimen...  16 us
    dot_general x2, matrix products, dense_plan(): jnp.dot(code_hot[t], vectors, preferred_element_type=jnp.float32)  15.4 us
    dot_general x3, matrix products, pair_counts(): lax.dot_general(left, right, (((2,), (2,)), ((0,), (0,))), preferred_elem...  15.3 us
    reshape x2, local copies, waits for them, and re-layouts, pair_counts(): tables = tables.reshape(groups, high, listed, low)  12 us
  transfers between devices with their start and end apart: 4, of which 3 were waited for; matrix products, arithmetic and copies ran while one was open for 43% of the time, Pallas kernels for 0%

profile of v1, /device:TPU:0, one launch (start us, length us, event | category | flops | bytes accessed | tf_op | source)
XLA Modules:
  0.0 309.2 jit_solution(4375504853129391879)
XLA Ops:
  9.4 7.1 %convolution_subtract_fusion.2 = f32[32,768]{1,0:T(8,128)} fusion(f32[32,768]{1,0:T(8,128)S(1)} %fusion.63, f32[32,2048]{1,0:T(8,128)S(1)} %bitcast.126, f32[2048,768]{1,0:T(8,128)} %param.11), kind=kOutput, calls=%fused_computation.56 | convolution fusion | flops 604004352 | bytes 6750208 | tf_op jit(solution)/shard_map/dot_general | solution.py:109
  16.7 24.7 %all-gather.1 = s32[16,1,6208]{2,1,0:T(1,128)S(1)} all-gather(s32[1,1,6208]{2,1,0:T(1,128)S(1)} %reshape.306), channel_id=1, replica_groups=mesh['parts'=2,'cell'=16] {'cell'}, dimensions={0}, use_global_device_ids=true | all-gather | bytes 422144 | tf_op jit(solution)/shard_map/all_gather | solution.py:143
  41.4 2.8 copy.46
  46.4 3.6 %fusion.44 = (s32[16,1536]{0,1:T(8,128)}, pred[16,1,1536]{0,2,1:T(8,128)(4,1)S(1)}, s32[16,1536]{0,1:T(8,128)}) fusion(s32[16,2,3104]{0,2,1:T(8,128)} %bitcast.112, pred[16,1,1536]{0,2,1:T(8,128)(4,1)S(1)} %get-tuple-element.13), kind=kLoop, calls=%fused_computation.65 | loop fusion | flops 663552 | bytes 540672 | tf_op jit(solution)/shard_map/eq | solution.py:113
  54.5 7.2 %fusion.1 = f32[16,256,256]{2,1,0:T(8,128)S(1)} fusion(s32[16,1536]{1,0:T(8,128)S(1)} %copy.54, s32[16,1536]{1,0:T(8,128)S(1)} %copy.53), kind=kOutput, calls=%fused_computation.5 | convolution fusion | flops 3233808384 | bytes 4390912 | tf_op jit(solution)/shard_map/dot_general | solution.py:122
  61.6 3.8 %bitcast_reduce_fusion = (f32[16,32]{1,0:T(8,128)S(1)}, f32[8,256]{1,0:T(8,128)S(1)}) fusion(f32[16,8,32,256]{3,2,1,0:T(8,128)S(1)} %bitcast.119), kind=kLoop, calls=%fused_computation.18 | loop fusion | flops 2094592 | bytes 4204544 | tf_op jit(solution)/shard_map/reduce_sum | solution.py:165
  65.4 7.6 %fusion = f32[16,256,256]{2,1,0:T(8,128)S(1)} fusion(s32[16,1536]{1,0:T(8,128)S(1)} %copy.49, s32[16,1536]{1,0:T(8,128)S(1)} %copy.48), kind=kOutput, calls=%fused_computation.4 | convolution fusion | flops 3233808384 | bytes 4390912 | tf_op jit(solution)/shard_map/dot_general | solution.py:122
  73.0 3.3 %copy.52 = f32[16,32,8,256]{3,2,1,0:T(8,128)S(1)} copy(f32[16,32,8,256]{3,1,2,0:T(8,128)S(1)} %bitcast.106) | data formatting | bytes 8388608 | tf_op jit(solution)/shard_map/transpose | solution.py:126
  78.9 5.9 %fusion.6 = f32[2048,768]{1,0:T(8,128)S(1)} fusion(bf16[1536,768]{1,0:T(8,128)(2,1)S(1)} %copy-done, s32[1536]{0:T(1024)S(1)} %get-tuple-element.10), kind=kOutput, calls=%fused_computation.12 | convolution fusion | flops 4834983936 | bytes 8656896 | tf_op jit(solution)/shard_map/dot_general | solution.py:154
  84.8 2.6 copy-done.6
  87.4 12.1 %fusion.16 = f32[512,768]{1,0:T(8,128)} fusion(f32[2048,768]{1,0:T(8,128)S(1)} %bitcast.110, f32[2048,768]{1,0:T(8,128)S(1)} %fusion.6, pred[2048]{0:T(1024)(128)(4,1)S(1)} %select_compare_fusion, f32[512,2048]{1,0:T(8,128)S(1)} %bitcast.117, f32[2048]{0:T(1024)S(1)} %broadcast_maximum_fusion, f32[32,768]{1,0:T(8,128)S(1)} %fusion.62, ...), kind=kOutput, calls=%fused_computation.26 | convolution fusion | flops 9667477504 | bytes 18459136 | tf_op jit(solution)/shard_map/dot_general | solution.py:109
  99.5 3.0 reshape.291
  102.6 3.4 %copy.56 = f32[16,16,2,768]{3,2,1,0:T(2,128)} copy(f32[16,16,2,768]{3,2,0,1:T(2,128)} %bitcast.124) | data formatting | bytes 3145728 | tf_op jit(solution)/shard_map/transpose | solution.py:187
  105.9 3.1 %reshape.292 = f32[512,768]{1,0:T(8,128)} reshape(f32[16,16,2,768]{3,2,1,0:T(2,128)} %copy.56) | data formatting | bytes 3145728 | tf_op jit(solution)/shard_map/reshape | solution.py:189
  110.1 7.5 %copy.55 = f32[16,8,32,256]{3,1,2,0:T(8,128)} copy(f32[16,8,32,256]{3,2,1,0:T(8,128)} %bitcast.120) | data formatting | bytes 8388608 | tf_op jit(solution)/shard_map/reshape | solution.py:125
  118.1 6.3 %copy.67 = f32[64,8,8,256]{3,1,2,0:T(8,128)} copy(f32[64,8,8,256]{3,2,1,0:T(8,128)} %bitcast.121) | data formatting | bytes 8388608
  124.4 4.5 %copy.79 = f32[16,8,32,256]{3,1,0,2:T(8,128)} copy(f32[16,8,32,256]{3,2,1,0:T(8,128)S(1)} %bitcast.107) | data formatting | bytes 8388608 | tf_op jit(solution)/shard_map/reshape | solution.py:125
  128.9 3.2 %fusion.96 = (f32[8,256]{1,0:T(8,128)S(1)}, f32[16,32]{0,1:T(8,128)S(1)}) fusion(f32[16,8,32,256]{3,2,1,0:T(8,128)S(1)} %bitcast.108), kind=kLoop, calls=%fused_computation.168 | loop fusion | flops 2094592 | bytes 4204544 | tf_op jit(solution)/shard_map/reduce_sum | solution.py:164
  132.3 5.3 %reshape.293 = f32[16,16,2,2048]{3,0,2,1:T(8,128)} reshape(f32[16,32,8,256]{3,2,0,1:T(8,128)} %bitcast.122) | data formatting | bytes 8388608 | tf_op jit(solution)/shard_map/reshape | solution.py:126
  139.9 6.1 %fusion.104 = f32[32,512]{1,0:T(8,128)S(1)} fusion(f32[32,2048]{1,0:T(8,128)S(1)} %reshape.294, f32[512,2048]{1,0:T(8,128)} %bitcast.115), kind=kOutput, calls=%fused_computation.172 | convolution fusion | flops 402653184 | bytes 4521984 | tf_op jit(solution)/shard_map/dot_general | solution.py:109
  146.0 4.2 %convolution_divide_fusion = f32[512,768]{1,0:T(8,128)} fusion(f32[512,768]{1,0:T(8,128)} %all-gather.5.cloned.1.call-done, f32[512]{0:T(512)S(1)} %broadcast_maximum_fusion.3, s32[512]{0:T(512)S(1)} %fusion.91), kind=kOutput, calls=%fused_computation.33 | convolution fusion | flops 2416574464 | bytes 3149824 | tf_op jit(solution)/shard_map/dot_general | solution.py:109
  150.1 16.0 %reduce-scatter.3.cloned.1.call-done = f32[32,768]{1,0:T(8,128)} async-done(((f32[512,768]{1,0:T(8,128)}), f32[32,768]{1,0:T(8,128)}) %reduce-scatter.3.cloned.1.call-update) | async-done | bytes 98320 | tf_op jit(solution)/shard_map/reduce_scatter | solution.py:188
  169.5 9.5 %fusion.13 = f32[2048,768]{1,0:T(8,128)} fusion(f32[2048,768]{1,0:T(8,128)} %copy-done.6, bf16[1536,768]{1,0:T(8,128)(2,1)S(1)} %copy-done, s32[1536]{0:T(1024)S(1)} %get-tuple-element.6, pred[2048]{0:T(1024)(128)(4,1)S(1)} %broadcast_compare_fusion), kind=kOutput, calls=%fused_computation.22 | convolution fusion | flops 4836556800 | bytes 14950400 | tf_op jit(solution)/shard_map/dot_general | solution.py:154
  180.2 3.0 reshape.300
  184.9 3.6 %select_select_fusion = f32[512,768]{1,0:T(8,128)} fusion(f32[512,768]{1,0:T(8,128)} %param.10, f32[512,768]{1,0:T(8,128)S(1)} %fusion.60, f32[32,768]{1,0:T(8,128)S(1)} %reshape.301, f32[512]{0:T(512)S(1)} %broadcast_maximum_fusion.1, f32[512]{0:T(512)S(1)} %broadcast_maximum_fusion.2, pred[512]{0:T(512)(128)(4,1)S(1)} %broadcast_compare_fusion.1, ...), kind=kOutput, calls=%fused_computation.28 | convolution fusion | flops 152584192 | bytes 4822144 | tf_op jit(solution)/shard_map/dot_general | solution.py:109
  188.5 19.8 %all-gather.7.cloned.1.call-done = f32[512,768]{1,0:T(8,128)} async-done(((f32[32,768]{1,0:T(8,128)}), f32[512,768]{1,0:T(8,128)}) %all-gather.7.cloned.1.call-update) | async-done | bytes 1572880 | tf_op jit(solution)/shard_map/all_gather | solution.py:208
  208.3 3.0 reshape.302
  211.3 3.4 %copy.80 = f32[16,16,2,768]{3,2,0,1:T(2,128)} copy(f32[16,16,2,768]{3,2,1,0:T(2,128)} %reshape.302) | data formatting | bytes 3145728 | tf_op jit(solution)/shard_map/reshape | solution.py:210
  214.7 3.2 %reshape.303 = f32[512,768]{1,0:T(8,128)} reshape(f32[16,16,2,768]{3,2,1,0:T(2,128)} %bitcast.125) | data formatting | bytes 3145728 | tf_op jit(solution)/shard_map/reshape | solution.py:212
  217.9 78.9 %reduce-scatter.5.cloned.1.call-done = f32[128,768]{1,0:T(8,128)} async-done(((f32[2048,768]{1,0:T(8,128)}), f32[128,768]{1,0:T(8,128)}) %reduce-scatter.5.cloned.1.call-update) | async-done | bytes 393232 | tf_op jit(solution)/shard_map/reduce_scatter | solution.py:174
  296.8 2.7 fusion.31
  299.5 3.0 fusion.30
  (90 shorter events, 21.5 us)
Async XLA Ops:
  7.2 1.7 copy-start
  7.2 138.8 %all-gather.5.cloned.1.call-start = ((), (), s32[]{:S(2)}) async-start(), calls=%async_computation.3 | async-start | bytes 1671168 | tf_op jit(solution)/shard_map/all_gather | solution.py:157
  9.4 7.2 %copy-start.7 = (s32[2,1536]{1,0:T(2,128)S(1)}, s32[2,1536]{1,0:T(2,128)}, u32[]{:S(2)}) copy-start(s32[2,1536]{1,0:T(2,128)} %param.8) | copy-start | bytes 36868
  9.4 7.2 %copy-start.8 = (s32[2,1536]{1,0:T(2,128)S(1)}, s32[2,1536]{1,0:T(2,128)}, u32[]{:S(2)}) copy-start(s32[2,1536]{1,0:T(2,128)} %param.7) | copy-start | bytes 36868
  9.4 7.2 %copy-start.9 = (s32[2,32]{1,0:T(2,128)S(1)}, s32[2,32]{1,0:T(2,128)}, u32[]{:S(2)}) copy-start(s32[2,32]{1,0:T(2,128)} %param.9) | copy-start | bytes 772
  16.5 149.7 %reduce-scatter.3.cloned.1.call-start = ((), (), s32[]{:S(2)}) async-start(), calls=%async_computation.2 | async-start | bytes 1671168 | tf_op jit(solution)/shard_map/reduce_scatter | solution.py:188
  61.6 3.8 %copy-start.4 = (f32[16,256,256]{2,1,0:T(8,128)}, f32[16,256,256]{2,1,0:T(8,128)S(1)}, u32[]{:S(2)}) copy-start(f32[16,256,256]{2,1,0:T(8,128)S(1)} %fusion.1) | copy-start | bytes 12582916
  73.0 3.3 %copy-start.1 = (f32[16,256,256]{2,1,0:T(8,128)}, f32[16,256,256]{2,1,0:T(8,128)S(1)}, u32[]{:S(2)}) copy-start(f32[16,256,256]{2,1,0:T(8,128)S(1)} %fusion) | copy-start | bytes 12582916
  78.3 6.5 %copy-start.3 = (f32[64,8,8,256]{3,1,2,0:T(8,128)}, f32[64,8,8,256]{3,1,2,0:T(8,128)S(1)}, u32[]{:S(2)}) copy-start(f32[64,8,8,256]{3,1,2,0:T(8,128)S(1)} %copy.65) | copy-start | bytes 12582916
  78.4 9.1 %slice-start = ((s8[6291456]{0:T(1024)(128)(4,1)}), s8[4194304]{0:T(1024)(128)(4,1)S(1)}, s32[]{:S(2)}) async-start(s8[6291456]{0:T(1024)(128)(4,1)} %bitcast.109), calls=%async_computation.6 | async-start | bytes 8388608
  78.9 8.6 %slice-start.1 = ((s8[6291456]{0:T(1024)(128)(4,1)}), s8[2097152]{0:T(1024)(128)(4,1)S(1)}, s32[]{:S(2)}) async-start(s8[6291456]{0:T(1024)(128)(4,1)} %bitcast.109), calls=%async_computation.7 | async-start | bytes 4194304
  84.8 2.7 copy-start.6
  109.1 99.2 %all-gather.7.cloned.1.call-start = ((), (), s32[]{:S(2)}) async-start(), calls=%async_computation.5 | async-start | bytes 1671168 | tf_op jit(solution)/shard_map/all_gather | solution.py:208
  118.1 6.3 %copy-start.2 = (f32[16,256,256]{2,1,0:T(8,128)S(1)}, f32[16,256,256]{2,1,0:T(8,128)}, u32[]{:S(2)}) copy-start(f32[16,256,256]{2,1,0:T(8,128)} %copy-done.1) | copy-start | bytes 12582916
  169.5 127.3 %reduce-scatter.5.cloned.1.call-start = ((), (), s32[]{:S(2)}) async-start(), calls=%async_computation.4 | async-start | bytes 6684672 | tf_op jit(solution)/shard_map/reduce_scatter | solution.py:174
  296.8 2.7 copy-start.5
Sparse Core Ops, SparseCore 0:
  16.6 42.7 all-gather.4
  109.2 56.8 reduce-scatter.2
  169.6 38.6 all-gather.6
  212.6 84.0 reduce-scatter.4

commit v2 on v0

--- a/solution.py
+++ b/solution.py
@@ -1,6 +1,8 @@
 import jax
 import jax.numpy as jnp
 from jax import lax
+from jax.experimental import pallas as pl
+from jax.experimental.pallas import tpu as pltpu
 from jax.sharding import PartitionSpec as P
 
 
@@ -22,7 +24,7 @@
     )
 
 
-def per_device(vectors, row_slot, fine_codes, cell_list, coarse_in, fine_in):
+def routed_plan(vectors, row_slot, fine_codes, cell_list, coarse_in, fine_in):
     groups = lax.axis_size("cell")
     rows_here, feature = vectors.shape
     listed = cell_list.shape[1]
@@ -103,6 +105,486 @@
     return (coarse, fine_share)
 
 
+F32 = jnp.float32
+BF16 = jnp.bfloat16
+LOW = 256
+LANES = 128
+PARAMS = pltpu.CompilerParams(vmem_limit_bytes=56 * 2**20)
+VMEM = pl.BlockSpec(memory_space=pltpu.VMEM)
+SMEM = pl.BlockSpec(memory_space=pltpu.SMEM)
+
+
+def iota(shape, axis):
+    return lax.broadcasted_iota(jnp.int32, shape, axis)
+
+
+def matmul(left, right):
+    return jnp.dot(left, right, preferred_element_type=F32)
+
+
+def matmul_nt(left, right):
+    return lax.dot_general(left, right, (((1,), (1,)), ((), ())), preferred_element_type=F32)
+
+
+def split(values):
+    high = values.astype(BF16)
+    return high, (values - high.astype(F32)).astype(BF16)
+
+
+def hot_rows(codes, rows=LOW):
+    inside = jnp.where((codes >= 0) & (codes < rows), codes, -1)
+    inside = inside.astype(F32).astype(BF16)
+    row = iota((rows, codes.shape[1]), 0).astype(F32).astype(BF16)
+    return jnp.where(row == inside, jnp.ones((), BF16), jnp.zeros((), BF16))
+
+
+def pair_block(codes, slots, listed, high):
+    left = hot_rows((codes >> 8) * listed + slots, high * listed)
+    return matmul_nt(left, hot_rows(codes & (LOW - 1)))
+
+
+def own_kernel(listed, vectors, fine_codes, row_slot, fine_in, first_ref, second_ref, sums_ref):
+    codewords = fine_in.shape[0]
+    high = codewords // LOW
+    first = matmul(hot_rows(row_slot[0:1, :], listed), vectors[...])
+    second_ref[...] = matmul(hot_rows(row_slot[1:2, :], listed), vectors[...])
+    codes = fine_codes[0:1, :]
+    pairs = pair_block(codes, row_slot[0:1, :], listed, high)
+    for digit in range(high):
+        pairs_high, pairs_low = split(pairs[digit * listed : (digit + 1) * listed])
+        both = jnp.concatenate([pairs_high, pairs_low], axis=0)
+        book = fine_in[digit * LOW : (digit + 1) * LOW, :]
+        book_high, book_low = split(book)
+        taken = matmul(both, book_high) + matmul(both, book_low)
+        first = first - taken[:listed] - taken[listed:]
+    first_ref[...] = first
+
+    def block(at, carry):
+        start = pl.multiple_of(at * 2 * LOW, 2 * LOW)
+        hot = jnp.concatenate(
+            [hot_rows(codes - start), hot_rows(codes - start - LOW)], axis=0
+        )
+        sums_ref[pl.ds(start, 2 * LOW), :] = matmul(hot, vectors[...])
+        return carry
+
+    lax.fori_loop(0, codewords // (2 * LOW), block, 0)
+
+
+def tables_kernel(
+    groups,
+    slot_count,
+    me_ref,
+    codes_ref,
+    sums_ref,
+    first_ref,
+    second_ref,
+    share_ref,
+    fine_ref,
+    bracket_ref,
+    pairs_ref,
+    centers_ref,
+    code_info_ref,
+    entry_info_ref,
+    passes_ref,
+    table0,
+    table1,
+    cell0,
+    cell1,
+    wide,
+    terms,
+    permuted,
+):
+    me = me_ref[0]
+    codewords, feature = sums_ref.shape
+    listed = groups * slot_count
+    entries = groups * listed
+    high = codewords // LOW
+    half = codes_ref.shape[2] - LANES
+    share_rows = share_ref.shape[0]
+
+    def device_tables(device, carry):
+        at = device ^ me
+        for sweep, table in enumerate((table0, table1)):
+            block = jnp.zeros((high * listed, LOW), F32)
+            for part in range(2):
+                row = 2 * sweep + part
+                block = block + pair_block(
+                    codes_ref[at, row : row + 1, :half],
+                    codes_ref[at, row + 4 : row + 5, :half],
+                    listed,
+                    high,
+                )
+            rows = pl.ds(pl.multiple_of(device * listed, listed), listed)
+            for digit in range(high):
+                table[rows, digit * LOW : (digit + 1) * LOW] = block[
+                    digit * listed : (digit + 1) * listed
+                ]
+        return carry
+
+    lax.fori_loop(0, groups, device_tables, 0)
+    for device in range(groups):
+        at = device ^ me
+        for sweep, cell in enumerate((cell0, cell1)):
+            row = codes_ref[at, sweep : sweep + 1, half : half + listed]
+            cell[device * slot_count : (device + 1) * slot_count, :] = jnp.broadcast_to(
+                row, (slot_count, listed)
+            )
+
+    row_at = iota((entries, listed), 0)
+    owner_of = row_at // listed
+    slot_of = owner_of * slot_count + row_at % slot_count
+    is_slot = slot_of == iota((entries, listed), 1)
+    device_of = (row_at // slot_count) % groups
+
+    def entry_cells(cell):
+        tiled = jnp.concatenate([cell[...]] * groups, axis=0)
+        picked = jnp.sum(jnp.where(is_slot, tiled, 0), axis=1, keepdims=True)
+        return picked.astype(F32)
+
+    owner_col = owner_of[:, :1].astype(F32)
+    cells = [entry_cells(cell0), entry_cells(cell1)]
+    names = [cell + owner_col * 4096.0 for cell in cells]
+
+    entry_row = iota((entries, entries), 0)
+    natural = (
+        ((entry_row // slot_count) % groups) * listed
+        + (entry_row // listed) * slot_count
+        + entry_row % slot_count
+    )
+    order = (natural == iota((entries, entries), 1)).astype(BF16)
+    passes = jnp.where(
+        jnp.maximum(jnp.max(table0[...]), jnp.max(table1[...])) > LOW, 2, 1
+    ).astype(jnp.int32)
+    passes_ref[0] = passes
+    code_counts = [jnp.sum(table[...], axis=0, keepdims=True) for table in (table0, table1)]
+    entry_counts = []
+    for table in (table0, table1):
+        count_high, count_low = split(
+            jnp.broadcast_to(jnp.sum(table[...], axis=1, keepdims=True), (entries, LANES))
+        )
+        entry_counts.append(matmul(order, count_high) + matmul(order, count_low))
+    for digit in range(high):
+        columns = slice(digit * LOW, (digit + 1) * LOW)
+        table_high, table_low = split(table1[:, columns])
+        permuted[0, :, columns] = matmul(order, table_high).astype(BF16)
+        permuted[1, :, columns] = matmul(order, table_low).astype(BF16)
+
+    own_row = codes_ref[0, 0:1, half : half + listed].astype(F32)
+    own_row = own_row + (iota((1, listed), 1) // slot_count).astype(F32) * 4096.0
+    match = (names[0] == own_row).astype(BF16)
+    match = lax.dot_general(match, order, (((0,), (0,)), ((), ())), preferred_element_type=F32)
+    match = match.astype(BF16)
+    for digit in range(high):
+        columns = slice(digit * LOW, (digit + 1) * LOW)
+        table_high, table_low = split(table0[:, columns])
+        used = matmul(match, table_high) + matmul(match, table_low)
+        used_high, used_low = split(used)
+        wide[0:listed, columns] = used_high.astype(F32)
+        wide[listed : 2 * listed, columns] = used_low.astype(F32)
+    held = wide[0:listed, :] + wide[listed : 2 * listed, :]
+    held = jnp.sum(held, axis=1, keepdims=True)
+    wide[2 * listed : 2 * listed + 8, :] = jnp.broadcast_to(code_counts[0], (8, codewords))
+    wide[2 * listed + 8 : 2 * listed + 16, :] = jnp.broadcast_to(code_counts[1], (8, codewords))
+    wide[2 * listed + 16 :, :] = jnp.zeros((LANES - 2 * listed - 16, codewords), F32)
+    center_high, center_low = split(first_ref[...] / jnp.maximum(held, 1.0))
+    center_high = jnp.concatenate(
+        [center_high, center_high, jnp.zeros((LANES - 2 * listed, feature), BF16)], axis=0
+    )
+    center_low = jnp.concatenate(
+        [center_low, center_low, jnp.zeros((LANES - 2 * listed, feature), BF16)], axis=0
+    )
+    for digit in range(high):
+        rows = slice(digit * LOW, (digit + 1) * LOW)
+        columns = wide[:, rows].T
+        code_info_ref[rows, :] = columns
+        columns_high = columns.astype(BF16)
+        columns_high = jnp.where(
+            iota((LOW, LANES), 1) < 2 * listed, columns_high.astype(F32), 0.0
+        ).astype(BF16)
+        fine = sums_ref[rows, :] - (
+            matmul(columns_high, center_high) + matmul(columns_high, center_low)
+        )
+        fine_ref[rows, :] = fine
+        scaled = fine / jnp.maximum(columns[:, 2 * listed : 2 * listed + 1], 1.0)
+        terms[0, rows, :], terms[1, rows, :] = split(scaled)
+    mine = pl.ds(pl.multiple_of(me * share_rows, share_rows), share_rows)
+    empty = code_info_ref[mine, 2 * listed : 2 * listed + 1] == 0
+    share_high, share_low = split(share_ref[...])
+    terms[0, mine, :] = jnp.where(
+        empty, share_high.astype(F32), terms[0, mine, :].astype(F32)
+    ).astype(BF16)
+    terms[1, mine, :] = jnp.where(
+        empty, share_low.astype(F32), terms[1, mine, :].astype(F32)
+    ).astype(BF16)
+
+    own_entry = (is_slot & (device_of == me)).astype(BF16)
+    second_high, second_low = split(second_ref[...])
+    bracket_ref[...] = (
+        matmul(own_entry, second_high)
+        + matmul(own_entry, second_low)
+        - matmul(permuted[0], terms[0])
+        - matmul(permuted[0], terms[1])
+    )
+
+    @pl.when(passes > 1)
+    def _():
+        bracket_ref[...] -= matmul(permuted[1], terms[0])
+
+    same = (
+        jnp.broadcast_to(names[1], (entries, entries))
+        == jnp.broadcast_to(names[1], (entries, LANES)).T[0:1, :]
+    ).astype(BF16)
+    total_high, total_low = split(entry_counts[1])
+    totals = matmul(same, total_high) + matmul(same, total_low)
+    bracket_high, bracket_low = split(bracket_ref[...])
+    centers = matmul(same, bracket_high) + matmul(same, bracket_low)
+    centers = centers / jnp.maximum(totals[:, :1], 1.0)
+    centers_ref[0], centers_ref[1] = split(centers)
+
+    eye = (iota((LOW, LOW), 0) == iota((LOW, LOW), 1)).astype(BF16)
+    for digit in range(high):
+        rows = slice(digit * LOW, (digit + 1) * LOW)
+        for part in range(2):
+            pairs_ref[part, rows, :] = matmul_nt(eye, permuted[part, :, rows]).astype(BF16)
+    lane = iota((entries, LANES), 1)
+    info = jnp.where(lane == 0, entry_counts[0], entry_counts[1])
+    info = jnp.where(lane == 2, cells[0], info)
+    entry_info_ref[...] = jnp.where(lane == 3, cells[1], info)
+
+
+def last_kernel(
+    blocks,
+    cuts,
+    listed,
+    me_ref,
+    passes_ref,
+    vectors,
+    fine_codes,
+    pairs_ref,
+    centers_ref,
+    fine_ref,
+    code_info_ref,
+    bracket_ref,
+    *refs,
+):
+    outs, left = refs[:-1], refs[-1]
+    me = me_ref[0]
+    rows_here = vectors.shape[0]
+    entries = centers_ref.shape[1]
+    cell_rows = listed
+    share_rows = outs[0].shape[1] - cell_rows
+    codes = fine_codes[1:2, :]
+    for at, block in enumerate(blocks):
+        owner = me ^ block
+        rows = pl.ds(pl.multiple_of(owner * share_rows, share_rows), share_rows)
+        to = slice(at * share_rows, (at + 1) * share_rows)
+        left[to, :rows_here] = hot_rows(codes - owner * share_rows, share_rows)
+        left[to, rows_here : rows_here + entries] = -pairs_ref[0, rows, :]
+    start = 0
+    for cut, out in zip(cuts, outs):
+        columns = slice(start, start + cut)
+        start += cut
+        sums = (
+            matmul(left[:, :rows_here], vectors[:, columns])
+            + matmul(left[:, rows_here:], centers_ref[0, :, columns])
+            + matmul(left[:, rows_here:], centers_ref[1, :, columns])
+        )
+        for at, block in enumerate(blocks):
+            owner = me ^ block
+            rows = pl.ds(pl.multiple_of(owner * share_rows, share_rows), share_rows)
+            used = code_info_ref[rows, 2 * listed + 8 : 2 * listed + 9] > 0
+            out[at, :share_rows, :] = jnp.where(
+                used, sums[at * share_rows : (at + 1) * share_rows], fine_ref[rows, columns]
+            )
+            cells = pl.ds(pl.multiple_of(owner * cell_rows, cell_rows), cell_rows)
+            out[at, share_rows:, :] = bracket_ref[cells, columns]
+
+            @pl.when(passes_ref[0] > 1)
+            def _():
+                more = matmul(pairs_ref[1, rows, :], centers_ref[0, :, columns])
+                out[at, :share_rows, :] = jnp.where(
+                    used, out[at, :share_rows, :] - more, out[at, :share_rows, :]
+                )
+
+
+def final_kernel(
+    share_rows,
+    coarse_in,
+    fine_share,
+    first_sums,
+    last_sums,
+    code_info,
+    entry_info,
+    coarse_out,
+    fine_out,
+):
+    listed = first_sums.shape[0]
+    owner_cells, feature = coarse_in.shape
+    by_lane = entry_info[...].T
+    info = [by_lane[at : at + 1, :] for at in range(4)]
+    coarse = coarse_in[...]
+    for sweep, sums in enumerate((first_sums[...], last_sums[share_rows:, :])):
+        cell = info[2 + sweep].astype(jnp.int32)
+        hit = iota((owner_cells, listed), 0) == cell
+        counts = jnp.sum(jnp.where(hit, info[sweep], 0.0), axis=1, keepdims=True)
+        picks = hit.astype(BF16)
+        sums_high, sums_low = split(sums)
+        found = matmul(picks, sums_high) + matmul(picks, sums_low)
+        coarse = jnp.where(counts > 0, found / jnp.maximum(counts, 1.0), coarse)
+    coarse_out[...] = coarse
+    first_count = code_info[:, 2 * listed : 2 * listed + 1]
+    last_count = code_info[:, 2 * listed + 8 : 2 * listed + 9]
+    count = jnp.where(last_count > 0, last_count, first_count)
+    fine_out[...] = jnp.where(
+        count > 0, last_sums[:share_rows, :] / jnp.maximum(count, 1.0), fine_share[...]
+    )
+
+
+def exchange(values, step):
+    groups = lax.axis_size("cell")
+    return lax.ppermute(values, "cell", [(at, at ^ step) for at in range(groups)])
+
+
+def gather_relative(values):
+    groups = lax.axis_size("cell")
+    far = groups // 4
+    blocks = [values] + [exchange(values, 4 * step) for step in range(1, far)]
+    near = jnp.stack(blocks)
+    near = jnp.stack([near, exchange(near, 2)])
+    both = jnp.stack([near, exchange(near, 1)])
+    return both
+
+
+def dense_plan(vectors, row_slot, fine_codes, cell_list, coarse_in, fine_in):
+    groups = lax.axis_size("cell")
+    me = lax.axis_index("cell")
+    rows_here, feature = vectors.shape
+    listed = cell_list.shape[1]
+    slot_count = listed // groups
+    codewords = fine_in.shape[0]
+    share_rows = codewords // groups
+    entries = groups * listed
+    half = rows_here // 2
+    me_arr = me.reshape(1).astype(jnp.int32)
+
+    codes = jnp.concatenate([fine_codes.reshape(4, half), row_slot.reshape(4, half)], axis=0)
+    cells = jnp.pad(cell_list, ((0, 6), (0, LANES - listed)))
+    packed = jnp.concatenate([codes, cells], axis=1)
+    gathered = gather_relative(packed)
+    gathered = gathered.reshape(2, 2, groups // 4, 8, half + LANES)
+    gathered = gathered.transpose(2, 1, 0, 3, 4).reshape(groups, 8, half + LANES)
+
+    first, second, sums = pl.pallas_call(
+        lambda *refs: own_kernel(listed, *refs),
+        out_shape=(
+            jax.ShapeDtypeStruct((listed, feature), F32),
+            jax.ShapeDtypeStruct((listed, feature), F32),
+            jax.ShapeDtypeStruct((codewords, feature), F32),
+        ),
+        in_specs=[VMEM] * 4,
+        out_specs=[VMEM] * 3,
+        compiler_params=PARAMS,
+        cost_estimate=pl.CostEstimate(flops=6 * 10**9, bytes_accessed=15 * 10**6, transcendentals=0),
+        name="own_sums",
+    )(vectors, fine_codes, row_slot, fine_in)
+    first_own = lax.all_to_all(
+        first.reshape(groups, slot_count, feature), "cell", split_axis=0, concat_axis=0, tiled=True
+    ).reshape(listed, feature)
+
+    fine_share = lax.dynamic_slice_in_dim(fine_in, me * share_rows, share_rows, 0)
+    fine, bracket, pairs, centers, code_info, entry_info, passes = pl.pallas_call(
+        lambda *refs: tables_kernel(groups, slot_count, *refs),
+        out_shape=(
+            jax.ShapeDtypeStruct((codewords, feature), F32),
+            jax.ShapeDtypeStruct((entries, feature), F32),
+            jax.ShapeDtypeStruct((2, codewords, entries), BF16),
+            jax.ShapeDtypeStruct((2, entries, feature), BF16),
+            jax.ShapeDtypeStruct((codewords, LANES), F32),
+            jax.ShapeDtypeStruct((entries, LANES), F32),
+            jax.ShapeDtypeStruct((1,), jnp.int32),
+        ),
+        in_specs=[SMEM] + [VMEM] * 5,
+        out_specs=[VMEM] * 6 + [SMEM],
+        scratch_shapes=[
+            pltpu.VMEM((entries, codewords), F32),
+            pltpu.VMEM((entries, codewords), F32),
+            pltpu.VMEM((listed, listed), jnp.int32),
+            pltpu.VMEM((listed, listed), jnp.int32),
+            pltpu.VMEM((LANES, codewords), F32),
+            pltpu.VMEM((2, codewords, feature), BF16),
+            pltpu.VMEM((2, entries, codewords), BF16),
+        ],
+        compiler_params=PARAMS,
+        cost_estimate=pl.CostEstimate(flops=20 * 10**9, bytes_accessed=20 * 10**6, transcendentals=0),
+        name="tables",
+    )(me_arr, gathered, sums, first, second, fine_share)
+
+    cuts = (2 * feature // 3, feature // 3)
+
+    def last_terms(blocks):
+        return pl.pallas_call(
+            lambda *refs: last_kernel(blocks, cuts, listed, *refs),
+            out_shape=tuple(
+                jax.ShapeDtypeStruct((len(blocks), share_rows + listed, cut), F32) for cut in cuts
+            ),
+            in_specs=[SMEM] * 2 + [VMEM] * 7,
+            out_specs=[VMEM] * len(cuts),
+            scratch_shapes=[pltpu.VMEM((len(blocks) * share_rows, rows_here + entries), BF16)],
+            compiler_params=PARAMS,
+            cost_estimate=pl.CostEstimate(
+                flops=4 * 10**8 * len(blocks), bytes_accessed=20 * 10**6, transcendentals=0
+            ),
+            name="last_sums",
+        )(me_arr, passes, vectors, fine_codes, pairs, centers, fine, code_info, bracket)
+
+    far = groups // 4
+    away = last_terms([4 * z + 2 * y + 1 for y in (1, 0) for z in range(far)])
+    near = last_terms([4 * z + 2 * y for y in (1, 0) for z in range(far)])
+    total = []
+    for column in range(2):
+        got = exchange(away[column], 1)
+        sums_here = near[column] + got
+        other, kept = sums_here[:far], sums_here[far:]
+        if column == 0:
+            kept = kept + exchange(other, 2)
+            pieces = [kept[0]] + [exchange(kept[z], 4 * z) for z in range(1, far)]
+            total.append(sum(pieces[1:], pieces[0]))
+        else:
+            pairs_z = jnp.stack([other, kept], axis=1)
+            pieces = [pairs_z[0]] + [exchange(pairs_z[z], 4 * z) for z in range(1, far)]
+            summed = sum(pieces[1:], pieces[0])
+            total.append(summed[1] + exchange(summed[0], 2))
+    last_sums = jnp.concatenate(total, axis=1)
+
+    own_code = lax.dynamic_slice_in_dim(code_info, me * share_rows, share_rows, 0)
+    own_entry = lax.dynamic_slice_in_dim(entry_info, me * listed, listed, 0)
+    return pl.pallas_call(
+        lambda *refs: final_kernel(share_rows, *refs),
+        out_shape=(
+            jax.ShapeDtypeStruct(coarse_in.shape, F32),
+            jax.ShapeDtypeStruct((share_rows, feature), F32),
+        ),
+        in_specs=[VMEM] * 6,
+        out_specs=[VMEM] * 2,
+        compiler_params=PARAMS,
+        name="outputs",
+    )(coarse_in, fine_share, first_own, last_sums, own_code, own_entry)
+
+
+def fits_dense(mesh_groups, listed, codewords, rows_here):
+    entries = mesh_groups * listed
+    power = mesh_groups & (mesh_groups - 1) == 0 and mesh_groups >= 4
+    digits = codewords % (2 * LOW) == 0 and (codewords // LOW) * listed <= LOW
+    return power and digits and entries * codewords <= 2**20 and rows_here % (2 * LANES) == 0
+
+
+def per_device(vectors, row_slot, fine_codes, cell_list, coarse_in, fine_in):
+    groups = lax.axis_size("cell")
+    dense = fits_dense(groups, cell_list.shape[1], fine_in.shape[0], vectors.shape[0])
+    plan = dense_plan if dense else routed_plan
+    return plan(vectors, row_slot, fine_codes, cell_list, coarse_in, fine_in)
+
+
 def solution(mesh):
     return jax.shard_map(
         per_device,

time: 384 us -> 181 us (0.47)
  waiting for transfers between devices: 162 us -> 62.4 us
  Pallas kernels: 0 us -> 77 us
  blocking collectives: 63.3 us -> 0 us
  local copies, waits for them, and re-layouts: 41.6 us -> 9.6 us
  matrix products: 28.5 us -> 0 us
  other arithmetic: 36.8 us -> 9.1 us
  starting transfers between devices: 35.9 us -> 21.2 us
  between operations: 14.4 us -> 0.77 us
    reduce_scatter x1 -> x0, waiting for transfers between devices: 82.6 us -> none  [fine_update(): lax.psum_scatter(code_term(jnp.int32(0), lax.axis_size('cell') * share_ro...]
    pallas_call x0 -> x5, Pallas kernels: none -> 77 us  [the longest x1 30.2 us: dense_plan(): pl.pallas_call(lambda *refs: tables_kernel(groups, slot_count, *refs), ou...]
    psum x1 -> x0, blocking collectives: 63.3 us -> none  [per_device(): code_totals = lax.psum(code_tally(fine_codes[sweep], codewords), 'cell')]
    psum x1 -> x0, waiting for transfers between devices: 40.1 us -> none  [per_device(): full_sums = lax.psum(code_term(0, codewords), 'cell')]
    ppermute x0 -> x15, waiting for transfers between devices: none -> 35.8 us  [exchange(): lax.ppermute(values, 'cell', [(at, at ^ step) for at in range(groups)])]
    gather x6 -> x0, local copies, waits for them, and re-layouts: 33.2 us -> none  [the longest x2 19.3 us: per_device(): picked = jnp.take(fine_book, code_rows, axis=0)]
    all_to_all x8 -> x1, starting transfers between devices: 35.8 us -> 3.51 us  [dense_plan(): lax.all_to_all(first.reshape(groups, slot_count, feature), 'cell', split_...]
    dot_general x4 -> x0, matrix products: 28.5 us -> none  [the longest x2 21.5 us: code_term(): return jnp.dot(code_hot, fine_residual, preferred_element_type=jnp.float32)]
  transfers between devices with their start and end apart: 10 -> 16, of which waited for: 8 -> 8; matrix products, arithmetic and copies ran while one was open for 10% -> 8% of each run, Pallas kernels for 0% -> 16%
where the time goes in v2:
time: 181 us; the launch traced here: 180 us
  Pallas kernels  77 us (43%)
  waiting for transfers between devices  62.4 us (34%)
  starting transfers between devices  21.2 us (12%)
  local copies, waits for them, and re-layouts  9.6 us (5%)
  other arithmetic  9.1 us (5%)
    ppermute x15, waiting for transfers between devices, exchange(): lax.ppermute(values, 'cell', [(at, at ^ step) for at in range(groups)])  35.8 us
    pallas_call x1, Pallas kernels, dense_plan(): pl.pallas_call(lambda *refs: tables_kernel(groups, slot_count, *refs), ou...  30.2 us
    pallas_call x2, Pallas kernels, last_terms(): pl.pallas_call(lambda *refs: last_kernel(blocks, cuts, listed, *refs), ou...  28.6 us
    all_to_all x1, waiting for transfers between devices, dense_plan(): lax.all_to_all(first.reshape(groups, slot_count, feature), 'cell', split_...  26.6 us
    ppermute x15, starting transfers between devices, exchange(): lax.ppermute(values, 'cell', [(at, at ^ step) for at in range(groups)])  17.7 us
    pallas_call x1, Pallas kernels, dense_plan(): pl.pallas_call(lambda *refs: own_kernel(listed, *refs), out_shape=(jax.Sh...  14.2 us
    pallas_call x1, Pallas kernels, dense_plan(): pl.pallas_call(lambda *refs: final_kernel(share_rows, *refs), out_shape=(...  4.07 us
  transfers between devices with their start and end apart: 16, of which 8 were waited for; matrix products, arithmetic and copies ran while one was open for 8% of the time, Pallas kernels for 16%

profile of v2, /device:TPU:0, one launch (start us, length us, event | category | flops | bytes accessed | tf_op | source)
XLA Modules:
  0.0 180.1 jit_solution(95758592701692860)
XLA Ops:
  2.8 4.1 %collective-permute-start.1 = (s32[8,896]{1,0:T(8,128)S(1)}, s32[8,896]{1,0:T(8,128)S(1)}, u32[]{:S(2)}, u32[]{:S(2)}) collective-permute-start(s32[8,896]{1,0:T(8,128)S(1)} %get-tuple-element.43), channel_id=1, source_target_pairs={{0,8},{1,9},{2,10},{3,11},{4,12},{5,13},{6,14},{7,15},{8,0},{9,1},... | collective-permute-start | bytes 86024 | tf_op jit(solution)/shard_map/ppermute | solution.py:445
  6.9 1.6 collective-permute-start
  8.7 2.0 %collective-permute-done = s32[8,896]{1,0:T(8,128)S(1)} collective-permute-done((s32[8,896]{1,0:T(8,128)S(1)}, s32[8,896]{1,0:T(8,128)S(1)}, u32[]{:S(2)}, u32[]{:S(2)}) %collective-permute-start) | collective-permute-done | bytes 28704 | tf_op jit(solution)/shard_map/ppermute | solution.py:445
  10.8 3.4 %collective-permute-done.2 = s32[8,896]{1,0:T(8,128)S(1)} collective-permute-done((s32[8,896]{1,0:T(8,128)S(1)}, s32[8,896]{1,0:T(8,128)S(1)}, u32[]{:S(2)}, u32[]{:S(2)}) %collective-permute-start.2) | collective-permute-done | bytes 28704 | tf_op jit(solution)/shard_map/ppermute | solution.py:445
  14.1 1.6 collective-permute-start.3
  15.7 3.3 %collective-permute-done.3 = s32[4,8,896]{2,1,0:T(8,128)S(1)} collective-permute-done((s32[4,8,896]{2,1,0:T(8,128)S(1)}, s32[4,8,896]{2,1,0:T(8,128)S(1)}, u32[]{:S(2)}, u32[]{:S(2)}) %collective-permute-start.3) | collective-permute-done | bytes 114720 | tf_op jit(solution)/shard_map/ppermute | solution.py:445
  19.1 14.2 %own_sums.1 = (f32[32,768]{1,0:T(8,128)}, f32[32,768]{1,0:T(8,128)}, f32[2048,768]{1,0:T(8,128)}) custom-call(bf16[1536,768]{1,0:T(8,128)(2,1)} %refs_2_.5, s32[2,1536]{1,0:T(2,128)} %refs_3_.5, s32[2,1536]{1,0:T(2,128)} %refs_2_.3, f32[2048,768]{1,0:T(8,128)} %refs_3_.3), custom_call_target="tpu_custom_call" | custom-call | flops 6000000000 | bytes 15000000 | tf_op jit(solution)/shard_map/own_sums/pallas_call | solution.py:477
  33.4 1.8 constant_dynamic-slice_fusion.2.refs_5_.refs_1_
  35.1 0.8 pad_add_fusion
  35.9 30.2 %tables.1 = (f32[2048,768]{1,0:T(8,128)}, f32[512,768]{1,0:T(8,128)}, bf16[2,2048,512]{2,1,0:T(8,128)(2,1)}, bf16[2,512,768]{2,1,0:T(8,128)(2,1)}, f32[2048,128]...) custom-call(s32[1]{0:T(128)} %bitcast.refs_0_, s32[16,8,896]{2,1,0:T(8,128)} %bitcast.59, ...), custom_call_target="tpu_custom_call" | custom-call | flops 20000000000 | bytes 20000000 | tf_op jit(solution)/shard_map/tables/pallas_call | solution.py:495
  66.1 14.1 %last_sums.3 = (f32[8,160,512]{2,1,0:T(8,128)}, f32[8,160,256]{2,1,0:T(8,128)}) custom-call(s32[1]{0:T(128)} %bitcast.refs_0_, s32[1]{0:T(128)} %get-tuple-element.19.refs_1_, bf16[1536,768]{1,0:T(8,128)(2,1)} %refs_2_.5, s32[2,1536]{1,0:T(2,128)} %refs_3_.5, bf16[2,2048,512]{2,1,0:T(8,128)(2,1)} %get-tuple-element.20.refs_4_, ...), custom_call_target="tpu_custom_call" | custom-call | flops 3200000000 | bytes 20000000 | tf_op jit(solution)/shard_map/last_sums/pallas_call | solution.py:525
  80.8 14.4 %last_sums.2 = (f32[8,160,512]{2,1,0:T(8,128)}, f32[8,160,256]{2,1,0:T(8,128)}) custom-call(s32[1]{0:T(128)} %bitcast.refs_0_, s32[1]{0:T(128)} %get-tuple-element.19.refs_1_, bf16[1536,768]{1,0:T(8,128)(2,1)} %refs_2_.5, s32[2,1536]{1,0:T(2,128)} %refs_3_.5, bf16[2,2048,512]{2,1,0:T(8,128)(2,1)} %get-tuple-element.20.refs_4_, ...), custom_call_target="tpu_custom_call" | custom-call | flops 3200000000 | bytes 20000000 | tf_op jit(solution)/shard_map/last_sums/pallas_call | solution.py:525
  95.2 2.5 %add.40 = f32[8,160,512]{2,1,0:T(8,128)S(1)} add(f32[8,160,512]{2,1,0:T(8,128)} %get-tuple-element.25, f32[8,160,512]{2,1,0:T(8,128)S(1)} %collective-permute-done.5) | non-fusion elementwise | flops 655360 | bytes 7864320 | tf_op jit(solution)/shard_map/add | solution.py:546
  97.7 1.2 slice.57
  98.9 1.5 collective-permute-start.6
  100.8 0.8 copy-done
  101.6 1.0 fusion.8
  102.9 3.2 %collective-permute-start.12 = (f32[2,160,256]{2,1,0:T(8,128)}, f32[2,160,256]{2,1,0:T(8,128)}, u32[]{:S(2)}, u32[]{:S(2)}) collective-permute-start(f32[2,160,256]{2,1,0:T(8,128)} %get-tuple-element.35), channel_id=1, source_target_pairs={{0,8},{1,9},{2,10},{3,11},{4,12},{5,13},{6,14},{7,15},{8,0},{9,1},... | collective-permute-start | bytes 983048 | tf_op jit(solution)/shard_map/ppermute | solution.py:445
  106.7 3.5 %all-to-all-start = ((f32[16,2,768]{2,1,0:T(2,128)}), f32[16,2,768]{2,1,0:T(2,128)S(1)}, u32[]{:S(2)}, u32[]{:S(2)}) async-start(f32[16,2,768]{2,1,0:T(2,128)} %reshape.22), calls=%async_computation | async-start | bytes 196608 | tf_op jit(solution)/shard_map/all_to_all | solution.py:490
  110.3 26.6 %all-to-all-done = f32[16,2,768]{2,1,0:T(2,128)S(1)} async-done(((f32[16,2,768]{2,1,0:T(2,128)}), f32[16,2,768]{2,1,0:T(2,128)S(1)}, u32[]{:S(2)}, u32[]{:S(2)}) %all-to-all-start) | async-done | bytes 98336 | tf_op jit(solution)/shard_map/all_to_all | solution.py:490
  137.5 1.5 constant_dynamic-slice_fusion.1.refs_4_
  139.0 1.3 fusion.6
  140.3 1.3 collective-permute-start.14
  141.6 1.6 slice_add_fusion
  144.0 1.1 collective-permute-start.9
  145.1 1.7 collective-permute-start.8
  146.8 1.3 constant_dynamic-slice_fusion.refs_5_
  148.2 10.8 %collective-permute-done.7 = f32[160,512]{1,0:T(8,128)S(1)} collective-permute-done((f32[160,512]{1,0:T(8,128)S(1)}, f32[160,512]{1,0:T(8,128)S(1)}, u32[]{:S(2)}, u32[]{:S(2)}) %collective-permute-start.7) | collective-permute-done | bytes 327712 | tf_op jit(solution)/shard_map/ppermute | solution.py:445
  158.9 1.9 %collective-permute-done.9 = f32[160,512]{1,0:T(8,128)S(1)} collective-permute-done((f32[160,512]{1,0:T(8,128)S(1)}, f32[160,512]{1,0:T(8,128)S(1)}, u32[]{:S(2)}, u32[]{:S(2)}) %collective-permute-start.9) | collective-permute-done | bytes 327712 | tf_op jit(solution)/shard_map/ppermute | solution.py:445
  160.8 14.2 %collective-permute-done.8 = f32[160,512]{1,0:T(8,128)S(1)} collective-permute-done((f32[160,512]{1,0:T(8,128)S(1)}, f32[160,512]{1,0:T(8,128)S(1)}, u32[]{:S(2)}, u32[]{:S(2)}) %collective-permute-start.8) | collective-permute-done | bytes 327712 | tf_op jit(solution)/shard_map/ppermute | solution.py:445
  175.2 0.8 pad_maximum_fusion.refs_3_
  176.0 4.1 %outputs.1 = (f32[512,768]{1,0:T(8,128)}, f32[128,768]{1,0:T(8,128)}) custom-call(f32[512,768]{1,0:T(8,128)} %refs_0_.3, f32[128,768]{1,0:T(8,128)} %constant_dynamic-slice_fusion.2.refs_5_.refs_1_, f32[32,768]{1,0:T(8,128)} %reshape.23.refs_2_, f32[160,768]{1,0:T(8,128)} %pad_maximum_fusion.refs_3_, f32[128,128]{1,0:T(8,128)} %constant_dynamic-slice_fusion.1.refs_4_, ...), custom_call_target="tpu_custom_call" | custom-call | tf_op jit(solution)/shard_map/outputs/pallas_call | solution.py:561
  (34 shorter events, 6.1 us)
Async XLA Ops:
  2.8 6.0 %collective-permute-start.1 = (s32[8,896]{1,0:T(8,128)S(1)}, s32[8,896]{1,0:T(8,128)S(1)}, u32[]{:S(2)}, u32[]{:S(2)}) collective-permute-start(s32[8,896]{1,0:T(8,128)S(1)} %get-tuple-element.43), channel_id=1, source_target_pairs={{0,8},{1,9},{2,10},{3,11},{4,12},{5,13},{6,14},{7,15},{8,0},{9,1},... | collective-permute-start | bytes 86024 | tf_op jit(solution)/shard_map/ppermute | solution.py:445
  6.9 3.9 %collective-permute-start = (s32[8,896]{1,0:T(8,128)S(1)}, s32[8,896]{1,0:T(8,128)S(1)}, u32[]{:S(2)}, u32[]{:S(2)}) collective-permute-start(s32[8,896]{1,0:T(8,128)S(1)} %get-tuple-element.43), channel_id=1, source_target_pairs={{0,4},{1,5},{2,6},{3,7},{4,0},{5,1},{6,2},{7,3},{8,12},{9,13},{10,... | collective-permute-start | bytes 86024 | tf_op jit(solution)/shard_map/ppermute | solution.py:445
  8.5 5.7 %collective-permute-start.2 = (s32[8,896]{1,0:T(8,128)S(1)}, s32[8,896]{1,0:T(8,128)S(1)}, u32[]{:S(2)}, u32[]{:S(2)}) collective-permute-start(s32[8,896]{1,0:T(8,128)S(1)} %get-tuple-element.43), channel_id=1, source_target_pairs={{0,12},{1,13},{2,14},{3,15},{4,8},{5,9},{6,10},{7,11},{8,4},{9,5},... | collective-permute-start | bytes 86024 | tf_op jit(solution)/shard_map/ppermute | solution.py:445
  14.1 4.9 %collective-permute-start.3 = (s32[4,8,896]{2,1,0:T(8,128)S(1)}, s32[4,8,896]{2,1,0:T(8,128)S(1)}, u32[]{:S(2)}, u32[]{:S(2)}) collective-permute-start(s32[4,8,896]{2,1,0:T(8,128)S(1)} %get-tuple-element.41), channel_id=1, source_target_pairs={{0,2},{1,3},{2,0},{3,1},{4,6},{5,7},{6,4},{7,5},{8,10},{9,11},{10,... | collective-permute-start | bytes 344072 | tf_op jit(solution)/shard_map/ppermute | solution.py:445
  19.0 16.1 %collective-permute-start.4 = (s32[2,4,8,896]{3,2,0,1:T(8,128)S(1)}, s32[2,4,8,896]{3,2,0,1:T(8,128)S(1)}, u32[]{:S(2)}, u32[]{:S(2)}) collective-permute-start(s32[2,4,8,896]{3,2,0,1:T(8,128)S(1)} %get-tuple-element.39), channel_id=1, source_target_pairs={{0,1},{1,0},{2,3},{3,2},{4,5},{5,4},{6,7},{7,6},{8,9},{9,8},{10,11... | collective-permute-start | bytes 688136 | tf_op jit(solution)/shard_map/ppermute | solution.py:445
  80.2 15.0 %collective-permute-start.5 = (f32[8,160,512]{2,1,0:T(8,128)}, f32[8,160,512]{2,1,0:T(8,128)S(1)}, u32[]{:S(2)}, u32[]{:S(2)}) collective-permute-start(f32[8,160,512]{2,1,0:T(8,128)} %get-tuple-element.26), channel_id=1, source_target_pairs={{0,1},{1,0},{2,3},{3,2},{4,5},{5,4},{6,7},{7,6},{8,9},{9,8},{10,11... | collective-permute-start | bytes 7864328 | tf_op jit(solution)/shard_map/ppermute | solution.py:445
  80.7 19.7 %collective-permute-start.10 = (f32[8,160,256]{2,1,0:T(8,128)}, f32[8,160,256]{2,1,0:T(8,128)S(1)}, u32[]{:S(2)}, u32[]{:S(2)}) collective-permute-start(f32[8,160,256]{2,1,0:T(8,128)} %get-tuple-element.28), channel_id=1, source_target_pairs={{0,1},{1,0},{2,3},{3,2},{4,5},{5,4},{6,7},{7,6},{8,9},{9,8},{10,11... | collective-permute-start | bytes 3932168 | tf_op jit(solution)/shard_map/ppermute | solution.py:445
  97.7 2.7 %copy-start.1 = (f32[8,160,256]{2,1,0:T(8,128)S(1)}, f32[8,160,256]{2,1,0:T(8,128)}, u32[]{:S(2)}) copy-start(f32[8,160,256]{2,1,0:T(8,128)} %get-tuple-element.27) | copy-start | bytes 3932164
  98.9 42.7 %collective-permute-start.6 = (f32[4,160,512]{2,1,0:T(8,128)}, f32[4,160,512]{2,1,0:T(8,128)}, u32[]{:S(2)}, u32[]{:S(2)}) collective-permute-start(f32[4,160,512]{2,1,0:T(8,128)} %slice.57), channel_id=1, source_target_pairs={{0,2},{1,3},{2,0},{3,1},{4,6},{5,7},{6,4},{7,5},{8,10},{9,11},{10,... | collective-permute-start | bytes 3932168 | tf_op jit(solution)/shard_map/ppermute | solution.py:445
  100.7 0.8 copy-start
  100.7 5.3 %copy-start.2 = (f32[32,768]{1,0:T(8,128)S(1)}, f32[32,768]{1,0:T(8,128)}, u32[]{:S(2)}) copy-start(f32[32,768]{1,0:T(8,128)} %get-tuple-element.16.refs_3_) | copy-start | bytes 294916
  102.6 36.5 %collective-permute-start.11 = (f32[2,160,256]{2,1,0:T(8,128)}, f32[2,160,256]{2,1,0:T(8,128)}, u32[]{:S(2)}, u32[]{:S(2)}) collective-permute-start(f32[2,160,256]{2,1,0:T(8,128)} %get-tuple-element.33), channel_id=1, source_target_pairs={{0,4},{1,5},{2,6},{3,7},{4,0},{5,1},{6,2},{7,3},{8,12},{9,13},{10,... | collective-permute-start | bytes 983048 | tf_op jit(solution)/shard_map/ppermute | solution.py:445
  102.6 36.5 %collective-permute-start.13 = (f32[2,160,256]{2,1,0:T(8,128)}, f32[2,160,256]{2,1,0:T(8,128)}, u32[]{:S(2)}, u32[]{:S(2)}) collective-permute-start(f32[2,160,256]{2,1,0:T(8,128)} %get-tuple-element.34), channel_id=1, source_target_pairs={{0,12},{1,13},{2,14},{3,15},{4,8},{5,9},{6,10},{7,11},{8,4},{9,5},... | collective-permute-start | bytes 983048 | tf_op jit(solution)/shard_map/ppermute | solution.py:445
  102.9 36.2 %collective-permute-start.12 = (f32[2,160,256]{2,1,0:T(8,128)}, f32[2,160,256]{2,1,0:T(8,128)}, u32[]{:S(2)}, u32[]{:S(2)}) collective-permute-start(f32[2,160,256]{2,1,0:T(8,128)} %get-tuple-element.35), channel_id=1, source_target_pairs={{0,8},{1,9},{2,10},{3,11},{4,12},{5,13},{6,14},{7,15},{8,0},{9,1},... | collective-permute-start | bytes 983048 | tf_op jit(solution)/shard_map/ppermute | solution.py:445
  106.7 30.1 %all-to-all-start = ((f32[16,2,768]{2,1,0:T(2,128)}), f32[16,2,768]{2,1,0:T(2,128)S(1)}, u32[]{:S(2)}, u32[]{:S(2)}) async-start(f32[16,2,768]{2,1,0:T(2,128)} %reshape.22), calls=%async_computation | async-start | bytes 196608 | tf_op jit(solution)/shard_map/all_to_all | solution.py:490
  140.3 7.8 %collective-permute-start.14 = (f32[160,256]{1,0:T(8,128)S(1)}, f32[160,256]{1,0:T(8,128)S(1)}, u32[]{:S(2)}, u32[]{:S(2)}) collective-permute-start(f32[160,256]{1,0:T(8,128)S(1)} %slice_bitcast_fusion.6), channel_id=1, source_target_pairs={{0,2},{1,3},{2,0},{3,1},{4,6},{5,7},{6,4},{7,5},{8,10},{9,11},{10,... | collective-permute-start | bytes 491528 | tf_op jit(solution)/shard_map/ppermute | solution.py:445
  143.3 15.7 %collective-permute-start.7 = (f32[160,512]{1,0:T(8,128)S(1)}, f32[160,512]{1,0:T(8,128)S(1)}, u32[]{:S(2)}, u32[]{:S(2)}) collective-permute-start(f32[160,512]{1,0:T(8,128)S(1)} %get-tuple-element.30), channel_id=1, source_target_pairs={{0,4},{1,5},{2,6},{3,7},{4,0},{5,1},{6,2},{7,3},{8,12},{9,13},{10,... | collective-permute-start | bytes 983048 | tf_op jit(solution)/shard_map/ppermute | solution.py:445
  144.0 16.8 %collective-permute-start.9 = (f32[160,512]{1,0:T(8,128)S(1)}, f32[160,512]{1,0:T(8,128)S(1)}, u32[]{:S(2)}, u32[]{:S(2)}) collective-permute-start(f32[160,512]{1,0:T(8,128)S(1)} %get-tuple-element.31), channel_id=1, source_target_pairs={{0,12},{1,13},{2,14},{3,15},{4,8},{5,9},{6,10},{7,11},{8,4},{9,5},... | collective-permute-start | bytes 983048 | tf_op jit(solution)/shard_map/ppermute | solution.py:445
  145.1 29.9 %collective-permute-start.8 = (f32[160,512]{1,0:T(8,128)S(1)}, f32[160,512]{1,0:T(8,128)S(1)}, u32[]{:S(2)}, u32[]{:S(2)}) collective-permute-start(f32[160,512]{1,0:T(8,128)S(1)} %get-tuple-element.32), channel_id=1, source_target_pairs={{0,8},{1,9},{2,10},{3,11},{4,12},{5,13},{6,14},{7,15},{8,0},{9,1},... | collective-permute-start | bytes 983048 | tf_op jit(solution)/shard_map/ppermute | solution.py:445

commit v3 on v2

--- a/solution.py
+++ b/solution.py
@@ -173,6 +173,7 @@
 def tables_kernel(
     groups,
     slot_count,
+    owner_cells,
     me_ref,
     codes_ref,
     sums_ref,
@@ -182,6 +183,7 @@
     fine_ref,
     bracket_ref,
     pairs_ref,
+    rest_ref,
     centers_ref,
     code_info_ref,
     entry_info_ref,
@@ -203,7 +205,7 @@
     share_rows = share_ref.shape[0]
 
     def device_tables(device, carry):
-        at = device ^ me
+        at = device
         for sweep, table in enumerate((table0, table1)):
             block = jnp.zeros((high * listed, LOW), F32)
             for part in range(2):
@@ -223,7 +225,7 @@
 
     lax.fori_loop(0, groups, device_tables, 0)
     for device in range(groups):
-        at = device ^ me
+        at = device
         for sweep, cell in enumerate((cell0, cell1)):
             row = codes_ref[at, sweep : sweep + 1, half : half + listed]
             cell[device * slot_count : (device + 1) * slot_count, :] = jnp.broadcast_to(
@@ -243,7 +245,7 @@
 
     owner_col = owner_of[:, :1].astype(F32)
     cells = [entry_cells(cell0), entry_cells(cell1)]
-    names = [cell + owner_col * 4096.0 for cell in cells]
+    names = [cell + owner_col * float(owner_cells) for cell in cells]
 
     entry_row = iota((entries, entries), 0)
     natural = (
@@ -269,8 +271,8 @@
         permuted[0, :, columns] = matmul(order, table_high).astype(BF16)
         permuted[1, :, columns] = matmul(order, table_low).astype(BF16)
 
-    own_row = codes_ref[0, 0:1, half : half + listed].astype(F32)
-    own_row = own_row + (iota((1, listed), 1) // slot_count).astype(F32) * 4096.0
+    own_row = codes_ref[me, 0:1, half : half + listed].astype(F32)
+    own_row = own_row + (iota((1, listed), 1) // slot_count).astype(F32) * float(owner_cells)
     match = (names[0] == own_row).astype(BF16)
     match = lax.dot_general(match, order, (((0,), (0,)), ((), ())), preferred_element_type=F32)
     match = match.astype(BF16)
@@ -304,7 +306,9 @@
         fine = sums_ref[rows, :] - (
             matmul(columns_high, center_high) + matmul(columns_high, center_low)
         )
-        fine_ref[rows, :] = fine
+        fine_ref[rows, :] = jnp.where(
+            columns[:, 2 * listed + 8 : 2 * listed + 9] > 0, 0.0, fine
+        )
         scaled = fine / jnp.maximum(columns[:, 2 * listed : 2 * listed + 1], 1.0)
         terms[0, rows, :], terms[1, rows, :] = split(scaled)
     mine = pl.ds(pl.multiple_of(me * share_rows, share_rows), share_rows)
@@ -344,8 +348,8 @@
     eye = (iota((LOW, LOW), 0) == iota((LOW, LOW), 1)).astype(BF16)
     for digit in range(high):
         rows = slice(digit * LOW, (digit + 1) * LOW)
-        for part in range(2):
-            pairs_ref[part, rows, :] = matmul_nt(eye, permuted[part, :, rows]).astype(BF16)
+        pairs_ref[rows, :] = matmul_nt(eye, permuted[0, :, rows]).astype(BF16)
+        rest_ref[rows, :] = matmul_nt(eye, permuted[1, :, rows]).astype(BF16)
     lane = iota((entries, LANES), 1)
     info = jnp.where(lane == 0, entry_counts[0], entry_counts[1])
     info = jnp.where(lane == 2, cells[0], info)
@@ -353,58 +357,57 @@
 
 
 def last_kernel(
-    blocks,
-    cuts,
+    orders,
     listed,
     me_ref,
     passes_ref,
     vectors,
     fine_codes,
     pairs_ref,
+    rest_ref,
     centers_ref,
     fine_ref,
-    code_info_ref,
     bracket_ref,
+    _,
     *refs,
 ):
-    outs, left = refs[:-1], refs[-1]
+    outs, left, rest, sem = refs[:-3], refs[-3], refs[-2], refs[-1]
     me = me_ref[0]
     rows_here = vectors.shape[0]
-    entries = centers_ref.shape[1]
-    cell_rows = listed
-    share_rows = outs[0].shape[1] - cell_rows
+    share_rows = outs[0].shape[1] - listed
     codes = fine_codes[1:2, :]
-    for at, block in enumerate(blocks):
-        owner = me ^ block
-        rows = pl.ds(pl.multiple_of(owner * share_rows, share_rows), share_rows)
-        to = slice(at * share_rows, (at + 1) * share_rows)
-        left[to, :rows_here] = hot_rows(codes - owner * share_rows, share_rows)
-        left[to, rows_here : rows_here + entries] = -pairs_ref[0, rows, :]
-    start = 0
-    for cut, out in zip(cuts, outs):
-        columns = slice(start, start + cut)
-        start += cut
-        sums = (
-            matmul(left[:, :rows_here], vectors[:, columns])
-            + matmul(left[:, rows_here:], centers_ref[0, :, columns])
-            + matmul(left[:, rows_here:], centers_ref[1, :, columns])
-        )
-        for at, block in enumerate(blocks):
+    for order, out in zip(orders, outs):
+        for at, block in enumerate(order):
             owner = me ^ block
             rows = pl.ds(pl.multiple_of(owner * share_rows, share_rows), share_rows)
-            used = code_info_ref[rows, 2 * listed + 8 : 2 * listed + 9] > 0
-            out[at, :share_rows, :] = jnp.where(
-                used, sums[at * share_rows : (at + 1) * share_rows], fine_ref[rows, columns]
+            to = slice(at * share_rows, (at + 1) * share_rows)
+            left[to, :rows_here] = hot_rows(codes - owner * share_rows, share_rows)
+            left[to, rows_here:] = -pairs_ref[rows, :]
+        used = slice(0, len(order) * share_rows)
+        sums = (
+            matmul(left[used, :rows_here], vectors[...])
+            + matmul(left[used, rows_here:], centers_ref[0])
+            + matmul(left[used, rows_here:], centers_ref[1])
+        )
+        for at, block in enumerate(order):
+            owner = me ^ block
+            rows = pl.ds(pl.multiple_of(owner * share_rows, share_rows), share_rows)
+            out[at, :share_rows, :] = (
+                sums[at * share_rows : (at + 1) * share_rows] + fine_ref[rows, :]
             )
-            cells = pl.ds(pl.multiple_of(owner * cell_rows, cell_rows), cell_rows)
-            out[at, share_rows:, :] = bracket_ref[cells, columns]
-
-            @pl.when(passes_ref[0] > 1)
-            def _():
-                more = matmul(pairs_ref[1, rows, :], centers_ref[0, :, columns])
-                out[at, :share_rows, :] = jnp.where(
-                    used, out[at, :share_rows, :] - more, out[at, :share_rows, :]
-                )
+            cells = pl.ds(pl.multiple_of(owner * listed, listed), listed)
+            out[at, share_rows:, :] = bracket_ref[cells, :]
+
+    @pl.when(passes_ref[0] > 1)
+    def _():
+        copy = pltpu.make_async_copy(rest_ref, rest, sem)
+        copy.start()
+        copy.wait()
+        for order, out in zip(orders, outs):
+            for at, block in enumerate(order):
+                owner = me ^ block
+                rows = pl.ds(pl.multiple_of(owner * share_rows, share_rows), share_rows)
+                out[at, :share_rows, :] -= matmul(rest[rows, :], centers_ref[0])
 
 
 def final_kernel(
@@ -445,14 +448,22 @@
     return lax.ppermute(values, "cell", [(at, at ^ step) for at in range(groups)])
 
 
-def gather_relative(values):
-    groups = lax.axis_size("cell")
-    far = groups // 4
-    blocks = [values] + [exchange(values, 4 * step) for step in range(1, far)]
-    near = jnp.stack(blocks)
-    near = jnp.stack([near, exchange(near, 2)])
-    both = jnp.stack([near, exchange(near, 1)])
-    return both
+def block_orders(bits):
+    order = [0]
+    for bit in bits[::-1]:
+        order = [block + (1 << bit) for block in order] + order
+    half = len(order) // 2
+    return [block + 1 for block in order], order[:half], order[half:]
+
+
+def scatter_sums(away, other, kept, bits):
+    got = exchange(away, 1)
+    other, kept = other + got[: other.shape[0]], kept + got[other.shape[0] :]
+    for bit in bits[:-1]:
+        got = exchange(other, 1 << bit)
+        half = got.shape[0] // 2
+        other, kept = kept[:half] + got[:half], kept[half:] + got[half:]
+    return (kept + exchange(other, 1 << bits[-1]))[0]
 
 
 def dense_plan(vectors, row_slot, fine_codes, cell_list, coarse_in, fine_in):
@@ -470,9 +481,13 @@
     codes = jnp.concatenate([fine_codes.reshape(4, half), row_slot.reshape(4, half)], axis=0)
     cells = jnp.pad(cell_list, ((0, 6), (0, LANES - listed)))
     packed = jnp.concatenate([codes, cells], axis=1)
-    gathered = gather_relative(packed)
-    gathered = gathered.reshape(2, 2, groups // 4, 8, half + LANES)
-    gathered = gathered.transpose(2, 1, 0, 3, 4).reshape(groups, 8, half + LANES)
+    gathered = lax.all_to_all(
+        jnp.broadcast_to(packed[None], (groups, *packed.shape)),
+        "cell",
+        split_axis=0,
+        concat_axis=0,
+        tiled=True,
+    )
 
     first, second, sums = pl.pallas_call(
         lambda *refs: own_kernel(listed, *refs),
@@ -492,19 +507,20 @@
     ).reshape(listed, feature)
 
     fine_share = lax.dynamic_slice_in_dim(fine_in, me * share_rows, share_rows, 0)
-    fine, bracket, pairs, centers, code_info, entry_info, passes = pl.pallas_call(
-        lambda *refs: tables_kernel(groups, slot_count, *refs),
+    fine, bracket, pairs, rest, centers, code_info, entry_info, passes = pl.pallas_call(
+        lambda *refs: tables_kernel(groups, slot_count, coarse_in.shape[0], *refs),
         out_shape=(
             jax.ShapeDtypeStruct((codewords, feature), F32),
             jax.ShapeDtypeStruct((entries, feature), F32),
-            jax.ShapeDtypeStruct((2, codewords, entries), BF16),
+            jax.ShapeDtypeStruct((codewords, entries), BF16),
+            jax.ShapeDtypeStruct((codewords, entries), BF16),
             jax.ShapeDtypeStruct((2, entries, feature), BF16),
             jax.ShapeDtypeStruct((codewords, LANES), F32),
             jax.ShapeDtypeStruct((entries, LANES), F32),
             jax.ShapeDtypeStruct((1,), jnp.int32),
         ),
         in_specs=[SMEM] + [VMEM] * 5,
-        out_specs=[VMEM] * 6 + [SMEM],
+        out_specs=[VMEM] * 7 + [SMEM],
         scratch_shapes=[
             pltpu.VMEM((entries, codewords), F32),
             pltpu.VMEM((entries, codewords), F32),
@@ -519,41 +535,45 @@
         name="tables",
     )(me_arr, gathered, sums, first, second, fine_share)
 
-    cuts = (2 * feature // 3, feature // 3)
-
-    def last_terms(blocks):
-        return pl.pallas_call(
-            lambda *refs: last_kernel(blocks, cuts, listed, *refs),
+    cut = feature // 3
+    top = groups.bit_length() - 1
+    near_first = list(range(1, top))
+    far_first = near_first[1:] + near_first[:1]
+    total = []
+    for at, bits in enumerate((near_first, far_first, near_first)):
+        orders = block_orders(bits)
+        away, other, kept = pl.pallas_call(
+            lambda *refs: last_kernel(orders, listed, *refs),
+            grid=(1,),
             out_shape=tuple(
-                jax.ShapeDtypeStruct((len(blocks), share_rows + listed, cut), F32) for cut in cuts
+                jax.ShapeDtypeStruct((len(order), share_rows + listed, cut), F32)
+                for order in orders
             ),
-            in_specs=[SMEM] * 2 + [VMEM] * 7,
-            out_specs=[VMEM] * len(cuts),
-            scratch_shapes=[pltpu.VMEM((len(blocks) * share_rows, rows_here + entries), BF16)],
+            in_specs=[
+                SMEM,
+                SMEM,
+                pl.BlockSpec((rows_here, cut), lambda step, at=at: (0, at)),
+                VMEM,
+                VMEM,
+                pl.BlockSpec(memory_space=pl.ANY),
+                pl.BlockSpec((2, entries, cut), lambda step, at=at: (0, 0, at)),
+                pl.BlockSpec((codewords, cut), lambda step, at=at: (0, at)),
+                pl.BlockSpec((entries, cut), lambda step, at=at: (0, at)),
+                pl.BlockSpec(memory_space=pl.ANY),
+            ],
+            out_specs=[VMEM] * len(orders),
+            scratch_shapes=[
+                pltpu.VMEM((len(orders[0]) * share_rows, rows_here + entries), BF16),
+                pltpu.VMEM((codewords, entries), BF16),
+                pltpu.SemaphoreType.DMA,
+            ],
             compiler_params=PARAMS,
             cost_estimate=pl.CostEstimate(
-                flops=4 * 10**8 * len(blocks), bytes_accessed=20 * 10**6, transcendentals=0
+                flops=27 * 10**8, bytes_accessed=8 * 10**6, transcendentals=0
             ),
             name="last_sums",
-        )(me_arr, passes, vectors, fine_codes, pairs, centers, fine, code_info, bracket)
-
-    far = groups // 4
-    away = last_terms([4 * z + 2 * y + 1 for y in (1, 0) for z in range(far)])
-    near = last_terms([4 * z + 2 * y for y in (1, 0) for z in range(far)])
-    total = []
-    for column in range(2):
-        got = exchange(away[column], 1)
-        sums_here = near[column] + got
-        other, kept = sums_here[:far], sums_here[far:]
-        if column == 0:
-            kept = kept + exchange(other, 2)
-            pieces = [kept[0]] + [exchange(kept[z], 4 * z) for z in range(1, far)]
-            total.append(sum(pieces[1:], pieces[0]))
-        else:
-            pairs_z = jnp.stack([other, kept], axis=1)
-            pieces = [pairs_z[0]] + [exchange(pairs_z[z], 4 * z) for z in range(1, far)]
-            summed = sum(pieces[1:], pieces[0])
-            total.append(summed[1] + exchange(summed[0], 2))
+        )(me_arr, passes, vectors, fine_codes, pairs, rest, centers, fine, bracket, first_own)
+        total.append(scatter_sums(away, other, kept, bits))
     last_sums = jnp.concatenate(total, axis=1)
 
     own_code = lax.dynamic_slice_in_dim(code_info, me * share_rows, share_rows, 0)

time: 181 us -> 164 us (0.906)
  waiting for transfers between devices: 62.4 us -> 55.5 us
  other arithmetic: 9.1 us -> 3.39 us
  Pallas kernels: 77 us -> 71.7 us
  starting transfers between devices: 21.2 us -> 23.9 us
    all_to_all x1, waiting for transfers between devices: 26.6 us -> 7.31 us  [dense_plan(): lax.all_to_all(first.reshape(groups, slot_count, feature), 'cell', split_...]
    all_to_all x0 -> x1, waiting for transfers between devices: none -> 10.5 us  [dense_plan(): lax.all_to_all(jnp.broadcast_to(packed[None], (groups, *packed.shape)), '...]
    pallas_call x3 -> x4, Pallas kernels: 58.7 us -> 53.5 us  [the longest x1 30 us: dense_plan(): pl.pallas_call(lambda *refs: tables_kernel(groups, slot_count, coarse_in....]
    ppermute x15 -> x12, starting transfers between devices: 17.7 us -> 12.8 us  [exchange(): lax.ppermute(values, 'cell', [(at, at ^ step) for at in range(groups)])]
    all_to_all x1, starting transfers between devices: 3.51 us -> 7.39 us  [dense_plan(): lax.all_to_all(first.reshape(groups, slot_count, feature), 'cell', split_...]
    all_to_all x0 -> x1, starting transfers between devices: none -> 3.74 us  [dense_plan(): lax.all_to_all(jnp.broadcast_to(packed[None], (groups, *packed.shape)), '...]
    add x6 -> x9, other arithmetic: 5.73 us -> 2.43 us  [the longest x3 2.11 us: scatter_sums(): other, kept = (other + got[:other.shape[0]], kept + got[other.shape[0]:])]
    ppermute x15 -> x12, waiting for transfers between devices: 35.8 us -> 37.6 us  [exchange(): lax.ppermute(values, 'cell', [(at, at ^ step) for at in range(groups)])]
  transfers between devices with their start and end apart: 16 -> 14, of which waited for: 8 -> 7; matrix products, arithmetic and copies ran while one was open for 8% -> 5% of each run, Pallas kernels for 16% -> 10%
where the time goes in v3:
time: 164 us
  Pallas kernels  71.7 us (44%)
  waiting for transfers between devices  55.5 us (34%)
  starting transfers between devices  23.9 us (15%)
  local copies, waits for them, and re-layouts  8.5 us (5%)
  other arithmetic  3.39 us (2%)
    ppermute x12, waiting for transfers between devices, exchange(): lax.ppermute(values, 'cell', [(at, at ^ step) for at in range(groups)])  37.6 us
    pallas_call x1, Pallas kernels, dense_plan(): pl.pallas_call(lambda *refs: tables_kernel(groups, slot_count, coarse_in....  30 us
    pallas_call x3, Pallas kernels, dense_plan(): pl.pallas_call(lambda *refs: last_kernel(orders, listed, *refs), grid=(1,...  23.6 us
    pallas_call x1, Pallas kernels, dense_plan(): pl.pallas_call(lambda *refs: own_kernel(listed, *refs), out_shape=(jax.Sh...  14 us
    ppermute x12, starting transfers between devices, exchange(): lax.ppermute(values, 'cell', [(at, at ^ step) for at in range(groups)])  12.8 us
    all_to_all x1, waiting for transfers between devices, dense_plan(): lax.all_to_all(jnp.broadcast_to(packed[None], (groups, *packed.shape)), '...  10.5 us
    all_to_all x1, starting transfers between devices, dense_plan(): lax.all_to_all(first.reshape(groups, slot_count, feature), 'cell', split_...  7.39 us
    all_to_all x1, waiting for transfers between devices, dense_plan(): lax.all_to_all(first.reshape(groups, slot_count, feature), 'cell', split_...  7.31 us
  transfers between devices with their start and end apart: 14, of which 7 were waited for; matrix products, arithmetic and copies ran while one was open for 5% of the time, Pallas kernels for 10%

profile of v3, /device:TPU:0, one launch (start us, length us, event | category | flops | bytes accessed | tf_op | source)
XLA Modules:
  0.0 163.8 jit_solution(1107873095394601497)
XLA Ops:
  0.7 14.0 %own_sums.1 = (f32[32,768]{1,0:T(8,128)}, f32[32,768]{1,0:T(8,128)}, f32[2048,768]{1,0:T(8,128)}) custom-call(bf16[1536,768]{1,0:T(8,128)(2,1)} %refs_2_.7, s32[2,1536]{1,0:T(2,128)} %refs_3_.7, s32[2,1536]{1,0:T(2,128)} %refs_2_.4, f32[2048,768]{1,0:T(8,128)} %refs_3_.4), custom_call_target="tpu_custom_call" | custom-call | flops 6000000000 | bytes 15000000 | tf_op jit(solution)/shard_map/own_sums/pallas_call | solution.py:492
  14.7 1.6 reshape.20
  16.3 7.4 %all-to-all-start = ((f32[16,2,768]{2,1,0:T(2,128)}), f32[16,2,768]{2,1,0:T(2,128)S(1)}, u32[]{:S(2)}, u32[]{:S(2)}) async-start(f32[16,2,768]{2,1,0:T(2,128)} %reshape.20), calls=%async_computation | async-start | bytes 196608 | tf_op jit(solution)/shard_map/all_to_all | solution.py:505
  23.8 7.3 %all-to-all-done = f32[16,2,768]{2,1,0:T(2,128)S(1)} async-done(((f32[16,2,768]{2,1,0:T(2,128)}), f32[16,2,768]{2,1,0:T(2,128)S(1)}, u32[]{:S(2)}, u32[]{:S(2)}) %all-to-all-start) | async-done | bytes 98336 | tf_op jit(solution)/shard_map/all_to_all | solution.py:505
  31.1 0.8 broadcast_in_dim.2
  31.9 3.7 %all-to-all-start.1 = ((s32[16,8,896]{2,1,0:T(8,128)}), s32[16,8,896]{2,1,0:T(8,128)S(1)}, u32[]{:S(2)}, u32[]{:S(2)}) async-start(s32[16,8,896]{2,1,0:T(8,128)} %broadcast_in_dim.2), calls=%async_computation.1 | async-start | bytes 917504 | tf_op jit(solution)/shard_map/all_to_all | solution.py:484
  35.7 1.8 %constant_dynamic-slice_fusion.2.refs_5_.refs_1_ = f32[128,768]{1,0:T(8,128)} fusion(f32[2048,768]{1,0:T(8,128)} %refs_3_.4, s32[]{:T(128)S(6)} %select_n.7), kind=kLoop, calls=%fused_computation.28 | loop fusion | bytes 786436 | tf_op jit(solution)/shard_map/dynamic_slice | solution.py:509
  37.4 0.7 reshape.21.refs_9_.refs_2_
  38.1 10.5 %all-to-all-done.1.refs_1_ = s32[16,8,896]{2,1,0:T(8,128)S(1)} async-done(((s32[16,8,896]{2,1,0:T(8,128)}), s32[16,8,896]{2,1,0:T(8,128)S(1)}, u32[]{:S(2)}, u32[]{:S(2)}) %all-to-all-start.1) | async-done | bytes 458784 | tf_op jit(solution)/shard_map/all_to_all | solution.py:484
  48.7 0.8 copy-done.5
  49.5 30.0 %tables.1 = (f32[2048,768]{1,0:T(8,128)}, f32[512,768]{1,0:T(8,128)}, bf16[2048,512]{1,0:T(8,128)(2,1)}, bf16[2048,512]{1,0:T(8,128)(2,1)}, bf16[2,512,768]{2,1,...) custom-call(s32[1]{0:T(128)} %bitcast.refs_0_, s32[16,8,896]{2,1,0:T(8,128)} %copy-done.5, ...), custom_call_target="tpu_custom_call" | custom-call | flops 20000000000 | bytes 20000000 | tf_op jit(solution)/shard_map/tables/pallas_call | solution.py:510
  79.5 7.8 %last_sums.3 = (f32[8,160,256]{2,1,0:T(8,128)}, f32[4,160,256]{2,1,0:T(8,128)}, f32[4,160,256]{2,1,0:T(8,128)}) custom-call(s32[1]{0:T(128)} %bitcast.refs_0_, s32[1]{0:T(128)} %get-tuple-element.25.refs_1_, bf16[1536,768]{1,0:T(8,128)(2,1)} %refs_2_.7, s32[2,1536]{1,0:T(2,128)} %refs_3_.7, bf16[2048,512]{1,0:T(8,128)(2,1)} %get-tuple-element.26.refs_4_, ...), custom_call_target="tpu_custom_call" | custom-call | flops 2700000000 | bytes 8000000 | tf_op jit(solution)/shard_map/last_sums/pallas_call | solution.py:545
  87.4 7.8 %last_sums.4 = (f32[8,160,256]{2,1,0:T(8,128)}, f32[4,160,256]{2,1,0:T(8,128)}, f32[4,160,256]{2,1,0:T(8,128)}) custom-call(s32[1]{0:T(128)} %bitcast.refs_0_, s32[1]{0:T(128)} %get-tuple-element.25.refs_1_, bf16[1536,768]{1,0:T(8,128)(2,1)} %refs_2_.7, s32[2,1536]{1,0:T(2,128)} %refs_3_.7, bf16[2048,512]{1,0:T(8,128)(2,1)} %get-tuple-element.26.refs_4_, ...), custom_call_target="tpu_custom_call" | custom-call | flops 2700000000 | bytes 8000000 | tf_op jit(solution)/shard_map/last_sums/pallas_call | solution.py:545
  95.7 8.0 %last_sums.5 = (f32[8,160,256]{2,1,0:T(8,128)}, f32[4,160,256]{2,1,0:T(8,128)}, f32[4,160,256]{2,1,0:T(8,128)}) custom-call(s32[1]{0:T(128)} %bitcast.refs_0_, s32[1]{0:T(128)} %get-tuple-element.25.refs_1_, bf16[1536,768]{1,0:T(8,128)(2,1)} %refs_2_.7, s32[2,1536]{1,0:T(2,128)} %refs_3_.7, bf16[2048,512]{1,0:T(8,128)(2,1)} %get-tuple-element.26.refs_4_, ...), custom_call_target="tpu_custom_call" | custom-call | flops 2700000000 | bytes 8000000 | tf_op jit(solution)/shard_map/last_sums/pallas_call | solution.py:545
  103.9 1.8 %slice_add_fusion.5 = (f32[4,160,256]{2,1,0:T(8,128)S(1)}, f32[4,160,256]{2,1,0:T(8,128)S(1)}) fusion(f32[4,160,256]{2,1,0:T(8,128)} %get-tuple-element.31, f32[8,160,256]{2,1,0:T(8,128)} %collective-permute-done, f32[4,160,256]{2,1,0:T(8,128)S(1)} %copy-done.4), kind=kLoop, calls=%fused_computation.5 | loop fusion | flops 327680 | bytes 3932160 | tf_op jit(solution)/shard_map/add | solution.py:461
  105.7 1.0 collective-permute-start.1
  106.9 1.4 collective-permute-start.5
  108.5 1.2 collective-permute-start.9
  109.7 1.3 constant_dynamic-slice_fusion.refs_5_
  111.0 1.5 constant_dynamic-slice_fusion.1.refs_4_
  112.5 10.8 %collective-permute-done.1 = f32[4,160,256]{2,1,0:T(8,128)S(1)} collective-permute-done((f32[4,160,256]{2,1,0:T(8,128)S(1)}, f32[4,160,256]{2,1,0:T(8,128)S(1)}, u32[]{:S(2)}, u32[]{:S(2)}) %collective-permute-start.1) | collective-permute-done | bytes 655392 | tf_op jit(solution)/shard_map/ppermute | solution.py:448
  123.4 1.5 collective-permute-start.2
  125.0 0.9 collective-permute-start.6
  125.9 10.9 %collective-permute-done.9 = f32[4,160,256]{2,1,0:T(8,128)S(1)} collective-permute-done((f32[4,160,256]{2,1,0:T(8,128)S(1)}, f32[4,160,256]{2,1,0:T(8,128)S(1)}, u32[]{:S(2)}, u32[]{:S(2)}) %collective-permute-start.9) | collective-permute-done | bytes 655392 | tf_op jit(solution)/shard_map/ppermute | solution.py:448
  136.9 1.2 collective-permute-start.10
  138.1 1.0 collective-permute-done.2
  139.2 2.9 %collective-permute-start.7 = (f32[1,160,256]{2,1,0:T(8,128)S(1)}, f32[1,160,256]{2,1,0:T(8,128)S(1)}, u32[]{:S(2)}, u32[]{:S(2)}) collective-permute-start(f32[1,160,256]{2,1,0:T(8,128)S(1)} %slice_add_fusion.14), channel_id=1, source_target_pairs={{0,2},{1,3},{2,0},{3,1},{4,6},{5,7},{6,4},{7,5},{8,10},{9,11},{10,... | collective-permute-start | bytes 491528 | tf_op jit(solution)/shard_map/ppermute | solution.py:448
  142.1 7.5 %collective-permute-done.10 = f32[2,160,256]{2,1,0:T(8,128)S(1)} collective-permute-done((f32[2,160,256]{2,1,0:T(8,128)S(1)}, f32[2,160,256]{2,1,0:T(8,128)S(1)}, u32[]{:S(2)}, u32[]{:S(2)}) %collective-permute-start.10) | collective-permute-done | bytes 327712 | tf_op jit(solution)/shard_map/ppermute | solution.py:448
  149.6 1.7 %collective-permute-start.11 = (f32[1,160,256]{2,1,0:T(8,128)S(1)}, f32[1,160,256]{2,1,0:T(8,128)S(1)}, u32[]{:S(2)}, u32[]{:S(2)}) collective-permute-start(f32[1,160,256]{2,1,0:T(8,128)S(1)} %slice_add_fusion.12), channel_id=1, source_target_pairs={{0,8},{1,9},{2,10},{3,11},{4,12},{5,13},{6,14},{7,15},{8,0},{9,1},... | collective-permute-start | bytes 491528 | tf_op jit(solution)/shard_map/ppermute | solution.py:448
  151.5 7.4 %collective-permute-done.11 = f32[1,160,256]{2,1,0:T(8,128)S(1)} collective-permute-done((f32[1,160,256]{2,1,0:T(8,128)S(1)}, f32[1,160,256]{2,1,0:T(8,128)S(1)}, u32[]{:S(2)}, u32[]{:S(2)}) %collective-permute-start.11) | collective-permute-done | bytes 163872 | tf_op jit(solution)/shard_map/ppermute | solution.py:448
  158.9 0.8 pad_maximum_fusion.refs_3_
  159.7 4.1 %outputs.1 = (f32[512,768]{1,0:T(8,128)}, f32[128,768]{1,0:T(8,128)}) custom-call(f32[512,768]{1,0:T(8,128)} %refs_0_.3, f32[128,768]{1,0:T(8,128)} %constant_dynamic-slice_fusion.2.refs_5_.refs_1_, f32[32,768]{1,0:T(8,128)} %reshape.21.refs_9_.refs_2_, f32[160,768]{1,0:T(8,128)} %pad_maximum_fusion.refs_3_, ...), custom_call_target="tpu_custom_call" | custom-call | tf_op jit(solution)/shard_map/outputs/pallas_call | solution.py:581
  (42 shorter events, 1.8 us)
Async XLA Ops:
  0.6 23.1 %copy-start.7 = (s32[2,1536]{1,0:T(2,128)S(1)}, s32[2,1536]{1,0:T(2,128)}, u32[]{:S(2)}) copy-start(s32[2,1536]{1,0:T(2,128)} %refs_2_.4) | copy-start | bytes 36868
  0.6 23.1 %copy-start.6 = (s32[2,1536]{1,0:T(2,128)S(1)}, s32[2,1536]{1,0:T(2,128)}, u32[]{:S(2)}) copy-start(s32[2,1536]{1,0:T(2,128)} %refs_3_.7) | copy-start | bytes 36868
  0.7 23.1 %copy-start.8 = (s32[2,32]{1,0:T(2,128)S(1)}, s32[2,32]{1,0:T(2,128)}, u32[]{:S(2)}) copy-start(s32[2,32]{1,0:T(2,128)} %param.9) | copy-start | bytes 772
  16.3 14.8 %all-to-all-start = ((f32[16,2,768]{2,1,0:T(2,128)}), f32[16,2,768]{2,1,0:T(2,128)S(1)}, u32[]{:S(2)}, u32[]{:S(2)}) async-start(f32[16,2,768]{2,1,0:T(2,128)} %reshape.20), calls=%async_computation | async-start | bytes 196608 | tf_op jit(solution)/shard_map/all_to_all | solution.py:505
  31.9 16.8 %all-to-all-start.1 = ((s32[16,8,896]{2,1,0:T(8,128)}), s32[16,8,896]{2,1,0:T(8,128)S(1)}, u32[]{:S(2)}, u32[]{:S(2)}) async-start(s32[16,8,896]{2,1,0:T(8,128)} %broadcast_in_dim.2), calls=%async_computation.1 | async-start | bytes 917504 | tf_op jit(solution)/shard_map/all_to_all | solution.py:484
  48.7 0.8 copy-start.5
  87.3 16.6 %collective-permute-start = (f32[8,160,256]{2,1,0:T(8,128)}, f32[8,160,256]{2,1,0:T(8,128)}, u32[]{:S(2)}, u32[]{:S(2)}) collective-permute-start(f32[8,160,256]{2,1,0:T(8,128)} %get-tuple-element.32), channel_id=1, source_target_pairs={{0,1},{1,0},{2,3},{3,2},{4,5},{5,4},{6,7},{7,6},{8,9},{9,8},{10,11... | collective-permute-start | bytes 3932168 | tf_op jit(solution)/shard_map/ppermute | solution.py:448
  95.2 8.7 %copy-start.4 = (f32[4,160,256]{2,1,0:T(8,128)S(1)}, f32[4,160,256]{2,1,0:T(8,128)}, u32[]{:S(2)}) copy-start(f32[4,160,256]{2,1,0:T(8,128)} %get-tuple-element.33) | copy-start | bytes 1966084
  95.2 11.5 %collective-permute-start.4 = (f32[8,160,256]{2,1,0:T(8,128)}, f32[8,160,256]{2,1,0:T(8,128)S(1)}, u32[]{:S(2)}, u32[]{:S(2)}) collective-permute-start(f32[8,160,256]{2,1,0:T(8,128)} %get-tuple-element.35), channel_id=1, source_target_pairs={{0,1},{1,0},{2,3},{3,2},{4,5},{5,4},{6,7},{7,6},{8,9},{9,8},{10,11... | collective-permute-start | bytes 3932168 | tf_op jit(solution)/shard_map/ppermute | solution.py:448
  103.7 4.6 %collective-permute-start.8 = (f32[8,160,256]{2,1,0:T(8,128)}, f32[8,160,256]{2,1,0:T(8,128)S(1)}, u32[]{:S(2)}, u32[]{:S(2)}) collective-permute-start(f32[8,160,256]{2,1,0:T(8,128)} %get-tuple-element.38), channel_id=1, source_target_pairs={{0,1},{1,0},{2,3},{3,2},{4,5},{5,4},{6,7},{7,6},{8,9},{9,8},{10,11... | collective-permute-start | bytes 3932168 | tf_op jit(solution)/shard_map/ppermute | solution.py:448
  103.9 2.8 %copy-start.2 = (f32[4,160,256]{2,1,0:T(8,128)S(1)}, f32[4,160,256]{2,1,0:T(8,128)}, u32[]{:S(2)}) copy-start(f32[4,160,256]{2,1,0:T(8,128)} %get-tuple-element.36) | copy-start | bytes 1966084
  103.9 2.8 %copy-start.3 = (f32[4,160,256]{2,1,0:T(8,128)S(1)}, f32[4,160,256]{2,1,0:T(8,128)}, u32[]{:S(2)}) copy-start(f32[4,160,256]{2,1,0:T(8,128)} %get-tuple-element.34) | copy-start | bytes 1966084
  105.7 17.6 %collective-permute-start.1 = (f32[4,160,256]{2,1,0:T(8,128)S(1)}, f32[4,160,256]{2,1,0:T(8,128)S(1)}, u32[]{:S(2)}, u32[]{:S(2)}) collective-permute-start(f32[4,160,256]{2,1,0:T(8,128)S(1)} %get-tuple-element.45), channel_id=1, source_target_pairs={{0,2},{1,3},{2,0},{3,1},{4,6},{5,7},{6,4},{7,5},{8,10},{9,11},{10,... | collective-permute-start | bytes 1966088 | tf_op jit(solution)/shard_map/ppermute | solution.py:448
  106.7 1.6 copy-start
  106.7 1.6 copy-start.1
  106.9 18.0 %collective-permute-start.5 = (f32[4,160,256]{2,1,0:T(8,128)S(1)}, f32[4,160,256]{2,1,0:T(8,128)S(1)}, u32[]{:S(2)}, u32[]{:S(2)}) collective-permute-start(f32[4,160,256]{2,1,0:T(8,128)S(1)} %get-tuple-element.49), channel_id=1, source_target_pairs={{0,4},{1,5},{2,6},{3,7},{4,0},{5,1},{6,2},{7,3},{8,12},{9,13},{10,... | collective-permute-start | bytes 1966088 | tf_op jit(solution)/shard_map/ppermute | solution.py:448
  108.5 28.3 %collective-permute-start.9 = (f32[4,160,256]{2,1,0:T(8,128)S(1)}, f32[4,160,256]{2,1,0:T(8,128)S(1)}, u32[]{:S(2)}, u32[]{:S(2)}) collective-permute-start(f32[4,160,256]{2,1,0:T(8,128)S(1)} %get-tuple-element.53), channel_id=1, source_target_pairs={{0,2},{1,3},{2,0},{3,1},{4,6},{5,7},{6,4},{7,5},{8,10},{9,11},{10,... | collective-permute-start | bytes 1966088 | tf_op jit(solution)/shard_map/ppermute | solution.py:448
  123.4 15.7 %collective-permute-start.2 = (f32[2,160,256]{2,1,0:T(8,128)S(1)}, f32[2,160,256]{2,1,0:T(8,128)S(1)}, u32[]{:S(2)}, u32[]{:S(2)}) collective-permute-start(f32[2,160,256]{2,1,0:T(8,128)S(1)} %get-tuple-element.43), channel_id=1, source_target_pairs={{0,4},{1,5},{2,6},{3,7},{4,0},{5,1},{6,2},{7,3},{8,12},{9,13},{10,... | collective-permute-start | bytes 983048 | tf_op jit(solution)/shard_map/ppermute | solution.py:448
  125.0 14.2 %collective-permute-start.6 = (f32[2,160,256]{2,1,0:T(8,128)S(1)}, f32[2,160,256]{2,1,0:T(8,128)S(1)}, u32[]{:S(2)}, u32[]{:S(2)}) collective-permute-start(f32[2,160,256]{2,1,0:T(8,128)S(1)} %get-tuple-element.47), channel_id=1, source_target_pairs={{0,8},{1,9},{2,10},{3,11},{4,12},{5,13},{6,14},{7,15},{8,0},{9,1},... | collective-permute-start | bytes 983048 | tf_op jit(solution)/shard_map/ppermute | solution.py:448
  136.9 12.7 %collective-permute-start.10 = (f32[2,160,256]{2,1,0:T(8,128)S(1)}, f32[2,160,256]{2,1,0:T(8,128)S(1)}, u32[]{:S(2)}, u32[]{:S(2)}) collective-permute-start(f32[2,160,256]{2,1,0:T(8,128)S(1)} %get-tuple-element.51), channel_id=1, source_target_pairs={{0,4},{1,5},{2,6},{3,7},{4,0},{5,1},{6,2},{7,3},{8,12},{9,13},{10,... | collective-permute-start | bytes 983048 | tf_op jit(solution)/shard_map/ppermute | solution.py:448
  139.1 12.3 %collective-permute-start.3 = (f32[1,160,256]{2,1,0:T(8,128)S(1)}, f32[1,160,256]{2,1,0:T(8,128)S(1)}, u32[]{:S(2)}, u32[]{:S(2)}) collective-permute-start(f32[1,160,256]{2,1,0:T(8,128)S(1)} %slice_add_fusion.16), channel_id=1, source_target_pairs={{0,8},{1,9},{2,10},{3,11},{4,12},{5,13},{6,14},{7,15},{8,0},{9,1},... | collective-permute-start | bytes 491528 | tf_op jit(solution)/shard_map/ppermute | solution.py:448
  139.2 12.2 %collective-permute-start.7 = (f32[1,160,256]{2,1,0:T(8,128)S(1)}, f32[1,160,256]{2,1,0:T(8,128)S(1)}, u32[]{:S(2)}, u32[]{:S(2)}) collective-permute-start(f32[1,160,256]{2,1,0:T(8,128)S(1)} %slice_add_fusion.14), channel_id=1, source_target_pairs={{0,2},{1,3},{2,0},{3,1},{4,6},{5,7},{6,4},{7,5},{8,10},{9,11},{10,... | collective-permute-start | bytes 491528 | tf_op jit(solution)/shard_map/ppermute | solution.py:448
  149.6 9.2 %collective-permute-start.11 = (f32[1,160,256]{2,1,0:T(8,128)S(1)}, f32[1,160,256]{2,1,0:T(8,128)S(1)}, u32[]{:S(2)}, u32[]{:S(2)}) collective-permute-start(f32[1,160,256]{2,1,0:T(8,128)S(1)} %slice_add_fusion.12), channel_id=1, source_target_pairs={{0,8},{1,9},{2,10},{3,11},{4,12},{5,13},{6,14},{7,15},{8,0},{9,1},... | collective-permute-start | bytes 491528 | tf_op jit(solution)/shard_map/ppermute | solution.py:448

commit v4 on v3

--- a/solution.py
+++ b/solution.py
@@ -112,6 +112,7 @@
 PARAMS = pltpu.CompilerParams(vmem_limit_bytes=56 * 2**20)
 VMEM = pl.BlockSpec(memory_space=pltpu.VMEM)
 SMEM = pl.BlockSpec(memory_space=pltpu.SMEM)
+ANY = pl.BlockSpec(memory_space=pl.ANY)
 
 
 def iota(shape, axis):
@@ -143,13 +144,11 @@
     return matmul_nt(left, hot_rows(codes & (LOW - 1)))
 
 
-def own_kernel(listed, vectors, fine_codes, row_slot, fine_in, first_ref, second_ref, sums_ref):
-    codewords = fine_in.shape[0]
-    high = codewords // LOW
+def own_cells_kernel(listed, vectors, fine_codes, row_slot, fine_in, first_ref, second_ref):
+    high = fine_in.shape[0] // LOW
     first = matmul(hot_rows(row_slot[0:1, :], listed), vectors[...])
     second_ref[...] = matmul(hot_rows(row_slot[1:2, :], listed), vectors[...])
-    codes = fine_codes[0:1, :]
-    pairs = pair_block(codes, row_slot[0:1, :], listed, high)
+    pairs = pair_block(fine_codes[0:1, :], row_slot[0:1, :], listed, high)
     for digit in range(high):
         pairs_high, pairs_low = split(pairs[digit * listed : (digit + 1) * listed])
         both = jnp.concatenate([pairs_high, pairs_low], axis=0)
@@ -159,15 +158,18 @@
         first = first - taken[:listed] - taken[listed:]
     first_ref[...] = first
 
-    def block(at, carry):
-        start = pl.multiple_of(at * 2 * LOW, 2 * LOW)
+
+def own_codes_kernel(base, vectors, fine_codes, _, sums_ref):
+    codes = fine_codes[0:1, :] - base
+    for start in range(0, sums_ref.shape[0], 2 * LOW):
         hot = jnp.concatenate(
             [hot_rows(codes - start), hot_rows(codes - start - LOW)], axis=0
         )
-        sums_ref[pl.ds(start, 2 * LOW), :] = matmul(hot, vectors[...])
-        return carry
-
-    lax.fori_loop(0, codewords // (2 * LOW), block, 0)
+        sums_ref[start : start + 2 * LOW, :] = matmul(hot, vectors[...])
+
+
+def position(block, groups):
+    return (block & 1) * (groups // 2) + (block >> 1 & 1) * (groups // 4) + (block >> 2)
 
 
 def tables_kernel(
@@ -176,7 +178,8 @@
     owner_cells,
     me_ref,
     codes_ref,
-    sums_ref,
+    low_sums_ref,
+    high_sums_ref,
     first_ref,
     second_ref,
     share_ref,
@@ -197,7 +200,7 @@
     permuted,
 ):
     me = me_ref[0]
-    codewords, feature = sums_ref.shape
+    codewords, feature = fine_ref.shape
     listed = groups * slot_count
     entries = groups * listed
     high = codewords // LOW
@@ -205,7 +208,7 @@
     share_rows = share_ref.shape[0]
 
     def device_tables(device, carry):
-        at = device
+        at = position(device ^ me, groups)
         for sweep, table in enumerate((table0, table1)):
             block = jnp.zeros((high * listed, LOW), F32)
             for part in range(2):
@@ -225,7 +228,7 @@
 
     lax.fori_loop(0, groups, device_tables, 0)
     for device in range(groups):
-        at = device
+        at = position(device ^ me, groups)
         for sweep, cell in enumerate((cell0, cell1)):
             row = codes_ref[at, sweep : sweep + 1, half : half + listed]
             cell[device * slot_count : (device + 1) * slot_count, :] = jnp.broadcast_to(
@@ -271,7 +274,7 @@
         permuted[0, :, columns] = matmul(order, table_high).astype(BF16)
         permuted[1, :, columns] = matmul(order, table_low).astype(BF16)
 
-    own_row = codes_ref[me, 0:1, half : half + listed].astype(F32)
+    own_row = codes_ref[0, 0:1, half : half + listed].astype(F32)
     own_row = own_row + (iota((1, listed), 1) // slot_count).astype(F32) * float(owner_cells)
     match = (names[0] == own_row).astype(BF16)
     match = lax.dot_general(match, order, (((0,), (0,)), ((), ())), preferred_element_type=F32)
@@ -303,7 +306,9 @@
         columns_high = jnp.where(
             iota((LOW, LANES), 1) < 2 * listed, columns_high.astype(F32), 0.0
         ).astype(BF16)
-        fine = sums_ref[rows, :] - (
+        at = digit % (high // 2) * LOW
+        sums_ref = low_sums_ref if digit < high // 2 else high_sums_ref
+        fine = sums_ref[at : at + LOW, :] - (
             matmul(columns_high, center_high) + matmul(columns_high, center_low)
         )
         fine_ref[rows, :] = jnp.where(
@@ -421,12 +426,13 @@
     coarse_out,
     fine_out,
 ):
-    listed = first_sums.shape[0]
-    owner_cells, feature = coarse_in.shape
+    listed = entry_info.shape[0]
+    owner_cells, cut = coarse_in.shape
     by_lane = entry_info[...].T
     info = [by_lane[at : at + 1, :] for at in range(4)]
     coarse = coarse_in[...]
-    for sweep, sums in enumerate((first_sums[...], last_sums[share_rows:, :])):
+    own_first = first_sums[...].reshape(listed, cut)
+    for sweep, sums in enumerate((own_first, last_sums[share_rows:, :])):
         cell = info[2 + sweep].astype(jnp.int32)
         hit = iota((owner_cells, listed), 0) == cell
         counts = jnp.sum(jnp.where(hit, info[sweep], 0.0), axis=1, keepdims=True)
@@ -456,9 +462,7 @@
     return [block + 1 for block in order], order[:half], order[half:]
 
 
-def scatter_sums(away, other, kept, bits):
-    got = exchange(away, 1)
-    other, kept = other + got[: other.shape[0]], kept + got[other.shape[0] :]
+def scatter_sums(other, kept, bits):
     for bit in bits[:-1]:
         got = exchange(other, 1 << bit)
         half = got.shape[0] // 2
@@ -466,62 +470,87 @@
     return (kept + exchange(other, 1 << bits[-1]))[0]
 
 
+def local(kernel, shapes, in_specs, out_specs, scratch, flops, name, aliases=None):
+    return pl.pallas_call(
+        kernel,
+        out_shape=tuple(jax.ShapeDtypeStruct(shape, dtype) for shape, dtype in shapes),
+        grid_spec=pltpu.PrefetchScalarGridSpec(
+            num_scalar_prefetch=1,
+            grid=(1,),
+            in_specs=in_specs,
+            out_specs=out_specs,
+            scratch_shapes=scratch,
+        ),
+        input_output_aliases=aliases or {},
+        compiler_params=PARAMS,
+        cost_estimate=pl.CostEstimate(
+            flops=int(flops), bytes_accessed=10**6, transcendentals=0
+        ),
+        name=name,
+    )
+
+
+def block(shape, *place):
+    return pl.BlockSpec(
+        shape, lambda step, me: tuple(me[0] if at is None else at for at in place)
+    )
+
+
 def dense_plan(vectors, row_slot, fine_codes, cell_list, coarse_in, fine_in):
     groups = lax.axis_size("cell")
-    me = lax.axis_index("cell")
     rows_here, feature = vectors.shape
     listed = cell_list.shape[1]
     slot_count = listed // groups
+    owner_cells = coarse_in.shape[0]
     codewords = fine_in.shape[0]
     share_rows = codewords // groups
     entries = groups * listed
     half = rows_here // 2
-    me_arr = me.reshape(1).astype(jnp.int32)
+    me = lax.axis_index("cell").reshape(1).astype(jnp.int32)
 
     codes = jnp.concatenate([fine_codes.reshape(4, half), row_slot.reshape(4, half)], axis=0)
     cells = jnp.pad(cell_list, ((0, 6), (0, LANES - listed)))
     packed = jnp.concatenate([codes, cells], axis=1)
-    gathered = lax.all_to_all(
-        jnp.broadcast_to(packed[None], (groups, *packed.shape)),
-        "cell",
-        split_axis=0,
-        concat_axis=0,
-        tiled=True,
-    )
-
-    first, second, sums = pl.pallas_call(
-        lambda *refs: own_kernel(listed, *refs),
-        out_shape=(
-            jax.ShapeDtypeStruct((listed, feature), F32),
-            jax.ShapeDtypeStruct((listed, feature), F32),
-            jax.ShapeDtypeStruct((codewords, feature), F32),
-        ),
-        in_specs=[VMEM] * 4,
-        out_specs=[VMEM] * 3,
-        compiler_params=PARAMS,
-        cost_estimate=pl.CostEstimate(flops=6 * 10**9, bytes_accessed=15 * 10**6, transcendentals=0),
-        name="own_sums",
-    )(vectors, fine_codes, row_slot, fine_in)
-    first_own = lax.all_to_all(
-        first.reshape(groups, slot_count, feature), "cell", split_axis=0, concat_axis=0, tiled=True
-    ).reshape(listed, feature)
-
-    fine_share = lax.dynamic_slice_in_dim(fine_in, me * share_rows, share_rows, 0)
-    fine, bracket, pairs, rest, centers, code_info, entry_info, passes = pl.pallas_call(
-        lambda *refs: tables_kernel(groups, slot_count, coarse_in.shape[0], *refs),
-        out_shape=(
-            jax.ShapeDtypeStruct((codewords, feature), F32),
-            jax.ShapeDtypeStruct((entries, feature), F32),
-            jax.ShapeDtypeStruct((codewords, entries), BF16),
-            jax.ShapeDtypeStruct((codewords, entries), BF16),
-            jax.ShapeDtypeStruct((2, entries, feature), BF16),
-            jax.ShapeDtypeStruct((codewords, LANES), F32),
-            jax.ShapeDtypeStruct((entries, LANES), F32),
-            jax.ShapeDtypeStruct((1,), jnp.int32),
-        ),
-        in_specs=[SMEM] + [VMEM] * 5,
-        out_specs=[VMEM] * 7 + [SMEM],
-        scratch_shapes=[
+    first, second = local(
+        lambda me_ref, *refs: own_cells_kernel(listed, *refs),
+        [((listed, feature), F32)] * 2,
+        [VMEM] * 4,
+        [VMEM] * 2,
+        [],
+        5e9,
+        "own_cells",
+    )(me, vectors, fine_codes, row_slot, fine_in)
+    first_all = lax.all_gather(first.reshape(groups, slot_count, feature), "cell")
+    far = groups // 4
+    gathered = jnp.stack([packed] + [exchange(packed, 4 * step) for step in range(1, far)])
+    sums = []
+    for step, base in ((2, 0), (1, codewords // 2)):
+        sums += local(
+            lambda me_ref, *refs, base=base: own_codes_kernel(base, *refs),
+            [((codewords // 2, feature), F32)],
+            [VMEM, VMEM, ANY],
+            [VMEM],
+            [],
+            6e9,
+            "own_codes",
+        )(me, vectors, fine_codes, gathered)
+        gathered = jnp.concatenate([gathered, exchange(gathered, step)])
+
+    fine, bracket, pairs, rest, centers, code_info, entry_info, passes = local(
+        lambda *refs: tables_kernel(groups, slot_count, owner_cells, *refs),
+        [
+            ((codewords, feature), F32),
+            ((entries, feature), F32),
+            ((codewords, entries), BF16),
+            ((codewords, entries), BF16),
+            ((2, entries, feature), BF16),
+            ((codewords, LANES), F32),
+            ((entries, LANES), F32),
+            ((1,), jnp.int32),
+        ],
+        [VMEM] * 5 + [block((share_rows, feature), None, 0)],
+        [VMEM] * 7 + [SMEM],
+        [
             pltpu.VMEM((entries, codewords), F32),
             pltpu.VMEM((entries, codewords), F32),
             pltpu.VMEM((listed, listed), jnp.int32),
@@ -530,65 +559,67 @@
             pltpu.VMEM((2, codewords, feature), BF16),
             pltpu.VMEM((2, entries, codewords), BF16),
         ],
-        compiler_params=PARAMS,
-        cost_estimate=pl.CostEstimate(flops=20 * 10**9, bytes_accessed=20 * 10**6, transcendentals=0),
-        name="tables",
-    )(me_arr, gathered, sums, first, second, fine_share)
+        34e9,
+        "tables",
+    )(me, gathered, *sums, first, second, fine_in)
 
     cut = feature // 3
     top = groups.bit_length() - 1
     near_first = list(range(1, top))
     far_first = near_first[1:] + near_first[:1]
-    total = []
+    begun = []
     for at, bits in enumerate((near_first, far_first, near_first)):
         orders = block_orders(bits)
-        away, other, kept = pl.pallas_call(
+        ahead = begun[-2][1] if len(begun) > 1 else first_all
+        away, other, kept = local(
             lambda *refs: last_kernel(orders, listed, *refs),
-            grid=(1,),
-            out_shape=tuple(
-                jax.ShapeDtypeStruct((len(order), share_rows + listed, cut), F32)
-                for order in orders
-            ),
-            in_specs=[
+            [((len(order), share_rows + listed, cut), F32) for order in orders],
+            [
                 SMEM,
-                SMEM,
-                pl.BlockSpec((rows_here, cut), lambda step, at=at: (0, at)),
+                block((rows_here, cut), 0, at),
                 VMEM,
                 VMEM,
-                pl.BlockSpec(memory_space=pl.ANY),
-                pl.BlockSpec((2, entries, cut), lambda step, at=at: (0, 0, at)),
-                pl.BlockSpec((codewords, cut), lambda step, at=at: (0, at)),
-                pl.BlockSpec((entries, cut), lambda step, at=at: (0, at)),
-                pl.BlockSpec(memory_space=pl.ANY),
+                ANY,
+                block((2, entries, cut), 0, 0, at),
+                block((codewords, cut), 0, at),
+                block((entries, cut), 0, at),
+                ANY,
             ],
-            out_specs=[VMEM] * len(orders),
-            scratch_shapes=[
+            [VMEM] * len(orders),
+            [
                 pltpu.VMEM((len(orders[0]) * share_rows, rows_here + entries), BF16),
                 pltpu.VMEM((codewords, entries), BF16),
                 pltpu.SemaphoreType.DMA,
             ],
-            compiler_params=PARAMS,
-            cost_estimate=pl.CostEstimate(
-                flops=27 * 10**8, bytes_accessed=8 * 10**6, transcendentals=0
-            ),
-            name="last_sums",
-        )(me_arr, passes, vectors, fine_codes, pairs, rest, centers, fine, bracket, first_own)
-        total.append(scatter_sums(away, other, kept, bits))
-    last_sums = jnp.concatenate(total, axis=1)
-
-    own_code = lax.dynamic_slice_in_dim(code_info, me * share_rows, share_rows, 0)
-    own_entry = lax.dynamic_slice_in_dim(entry_info, me * listed, listed, 0)
-    return pl.pallas_call(
-        lambda *refs: final_kernel(share_rows, *refs),
-        out_shape=(
-            jax.ShapeDtypeStruct(coarse_in.shape, F32),
-            jax.ShapeDtypeStruct((share_rows, feature), F32),
-        ),
-        in_specs=[VMEM] * 6,
-        out_specs=[VMEM] * 2,
-        compiler_params=PARAMS,
-        name="outputs",
-    )(coarse_in, fine_share, first_own, last_sums, own_code, own_entry)
+            9e9,
+            "last_sums",
+        )(me, passes, vectors, fine_codes, pairs, rest, centers, fine, bracket, ahead)
+        got = exchange(away, 1)
+        size = other.shape[0]
+        begun.append((bits, other + got[:size], kept + got[size:]))
+
+    outs = ()
+    for at, (bits, other, kept) in enumerate(begun):
+        last_sums = scatter_sums(other, kept, bits)
+        outs = local(
+            lambda me_ref, *refs: final_kernel(share_rows, *refs[:6], *refs[-2:]),
+            [(coarse_in.shape, F32), ((share_rows, feature), F32)],
+            [
+                block((owner_cells, cut), 0, at),
+                block((share_rows, cut), None, at),
+                block((groups, 1, slot_count, cut), 0, None, 0, at),
+                VMEM,
+                block((share_rows, LANES), None, 0),
+                block((listed, LANES), None, 0),
+            ]
+            + [ANY] * len(outs),
+            [block((owner_cells, cut), 0, at), block((share_rows, cut), 0, at)],
+            [],
+            1e9,
+            "outputs",
+            {7 + number: number for number in range(len(outs))},
+        )(me, coarse_in, fine_in, first_all, last_sums, code_info, entry_info, *outs)
+    return tuple(outs)
 
 
 def fits_dense(mesh_groups, listed, codewords, rows_here):

time: 164 us -> 167 us (1.018)
  waiting for transfers between devices: 55.5 us -> 41 us
  between operations: 0.86 us -> 14.3 us
  Pallas kernels: 71.7 us -> 80.1 us
  starting transfers between devices: 23.9 us -> 18.1 us
    all_to_all x2 -> x0, waiting for transfers between devices: 17.9 us -> none  [the longest x1 10.5 us: dense_plan(): lax.all_to_all(jnp.broadcast_to(packed[None], (groups, *packed.shape)), '...]
    all_to_all x2 -> x0, starting transfers between devices: 11.1 us -> none  [the longest x1 7.39 us: dense_plan(): lax.all_to_all(first.reshape(groups, slot_count, feature), 'cell', split_...]
    pallas_call x6 -> x10, Pallas kernels: 71.7 us -> 80.1 us  [the longest x1 30.2 us: dense_plan(): local(lambda *refs: tables_kernel(groups, slot_count, owner_cells, *refs)...]
    ppermute x12 -> x17, starting transfers between devices: 12.8 us -> 18.1 us  [exchange(): lax.ppermute(values, 'cell', [(at, at ^ step) for at in range(groups)])]
    dynamic_slice x3 -> x0, local copies, waits for them, and re-layouts: 4.56 us -> none  [the longest x1 1.77 us: dense_plan(): lax.dynamic_slice_in_dim(fine_in, me * share_rows, share_rows, 0)]
    all_gather x0 -> x1, local copies, waits for them, and re-layouts: none -> 3.82 us  [dense_plan(): lax.all_gather(first.reshape(groups, slot_count, feature), 'cell')]
    ppermute x12 -> x17, waiting for transfers between devices: 37.6 us -> 41 us  [exchange(): lax.ppermute(values, 'cell', [(at, at ^ step) for at in range(groups)])]
    reshape x2 -> x0, local copies, waits for them, and re-layouts: 2.29 us -> none  [the longest x1 1.59 us: dense_plan(): first.reshape(groups, slot_count, feature)]
  transfers between devices with their start and end apart: 14 -> 18, of which waited for: 7 -> 7; matrix products, arithmetic and copies ran while one was open for 5% -> 3% of each run, Pallas kernels for 10% -> 42%
where the time goes in v4:
time: 167 us; the launch traced here: 166 us
  Pallas kernels  80.1 us (48%)
  waiting for transfers between devices  41 us (25%)
  starting transfers between devices  18.1 us (11%)
  between operations  14.3 us (9%)
  local copies, waits for them, and re-layouts  8.33 us (5%)
  other arithmetic  4.52 us (3%)
    ppermute x17, waiting for transfers between devices, exchange(): lax.ppermute(values, 'cell', [(at, at ^ step) for at in range(groups)])  41 us
    pallas_call x1, Pallas kernels, dense_plan(): local(lambda *refs: tables_kernel(groups, slot_count, owner_cells, *refs)...  30.2 us
    pallas_call x3, Pallas kernels, dense_plan(): local(lambda *refs: last_kernel(orders, listed, *refs), [((len(order), sh...  23.8 us
    ppermute x17, starting transfers between devices, exchange(): lax.ppermute(values, 'cell', [(at, at ^ step) for at in range(groups)])  18.1 us
    pallas_call x2, Pallas kernels, dense_plan(): local(lambda me_ref, *refs, base=base: own_codes_kernel(base, *refs), [((...  12 us
    pallas_call x3, Pallas kernels, dense_plan(): local(lambda me_ref, *refs: final_kernel(share_rows, *refs[:6], *refs[-2:...  7.5 us
    pallas_call x1, Pallas kernels, dense_plan(): local(lambda me_ref, *refs: own_cells_kernel(listed, *refs), [((listed, f...  6.55 us
    all_gather x1, local copies, waits for them, and re-layouts, dense_plan(): lax.all_gather(first.reshape(groups, slot_count, feature), 'cell')  3.82 us
  transfers between devices with their start and end apart: 18, of which 7 were waited for; matrix products, arithmetic and copies ran while one was open for 3% of the time, Pallas kernels for 42%

profile of v4, /device:TPU:0, one launch (start us, length us, event | category | flops | bytes accessed | tf_op | source)
XLA Modules:
  0.0 166.4 jit_solution(12066922850711991177)
XLA Ops:
  7.2 0.7 reshape.14
  7.9 0.7 reshape.15
  9.4 3.1 %collective-permute-start = (s32[8,896]{1,0:T(8,128)S(1)}, s32[8,896]{1,0:T(8,128)S(1)}, u32[]{:S(2)}, u32[]{:S(2)}) collective-permute-start(s32[8,896]{1,0:T(8,128)S(1)} %get-tuple-element.71), channel_id=1, source_target_pairs={{0,4},{1,5},{2,6},{3,7},{4,0},{5,1},{6,2},{7,3},{8,12},{9,13},{10,... | collective-permute-start | bytes 86024 | tf_op jit(solution)/shard_map/ppermute | solution.py:454
  12.4 2.6 %collective-permute-start.1 = (s32[8,896]{1,0:T(8,128)S(1)}, s32[8,896]{1,0:T(8,128)S(1)}, u32[]{:S(2)}, u32[]{:S(2)}) collective-permute-start(s32[8,896]{1,0:T(8,128)S(1)} %get-tuple-element.71), channel_id=1, source_target_pairs={{0,8},{1,9},{2,10},{3,11},{4,12},{5,13},{6,14},{7,15},{8,0},{9,1},... | collective-permute-start | bytes 86024 | tf_op jit(solution)/shard_map/ppermute | solution.py:454
  15.0 6.5 %own_cells.1 = (f32[32,768]{1,0:T(8,128)}, f32[32,768]{1,0:T(8,128)}) custom-call(s32[1]{0:T(128)} %bitcast.me_ref.refs_0_, bf16[1536,768]{1,0:T(8,128)(2,1)} %refs_2_.7, s32[2,1536]{1,0:T(2,128)} %refs_3_.7, s32[2,1536]{1,0:T(2,128)} %refs_2_.4, f32[2048,768]{1,0:T(8,128)} %refs_1_.11), custom_call_target="tpu_custom_call" | custom-call | flops 5000000000 | bytes 1000000 | tf_op jit(solution)/shard_map/own_cells/pallas_call | solution.py:514
  21.6 0.9 all_gather_reshape.3
  23.3 1.8 %collective-permute-start.3 = (s32[4,8,896]{2,1,0:T(8,128)S(1)}, s32[4,8,896]{2,1,0:T(8,128)S(1)}, u32[]{:S(2)}, u32[]{:S(2)}) collective-permute-start(s32[4,8,896]{2,1,0:T(8,128)S(1)} %pad_add_fusion.refs_2_), channel_id=1, source_target_pairs={{0,2},{1,3},{2,0},{3,1},{4,6},{5,7},{6,4},{7,5},{8,10},{9,11},{10,... | collective-permute-start | bytes 344072 | tf_op jit(solution)/shard_map/ppermute | solution.py:454
  25.1 6.0 %own_codes.2.refs_2_ = f32[1024,768]{1,0:T(8,128)} custom-call(s32[1]{0:T(128)} %bitcast.me_ref.refs_0_, bf16[1536,768]{1,0:T(8,128)(2,1)} %refs_2_.7, s32[2,1536]{1,0:T(2,128)} %refs_3_.7, s32[4,8,896]{2,1,0:T(8,128)} %copy-done.7), custom_call_target="tpu_custom_call" | custom-call | flops 6000000000 | bytes 1000000 | tf_op jit(solution)/shard_map/own_codes/pallas_call | solution.py:528
  31.8 6.0 %own_codes.3.refs_3_ = f32[1024,768]{1,0:T(8,128)} custom-call(s32[1]{0:T(128)} %bitcast.me_ref.refs_0_, bf16[1536,768]{1,0:T(8,128)(2,1)} %refs_2_.7, s32[2,1536]{1,0:T(2,128)} %refs_3_.7, s32[8,8,896]{2,1,0:T(8,128)} %copy-done.9), custom_call_target="tpu_custom_call" | custom-call | flops 6000000000 | bytes 1000000 | tf_op jit(solution)/shard_map/own_codes/pallas_call | solution.py:528
  37.9 0.8 copy-done.10
  38.7 30.2 %tables.1 = (f32[2048,768]{1,0:T(8,128)}, f32[512,768]{1,0:T(8,128)}, bf16[2048,512]{1,0:T(8,128)(2,1)}, bf16[2048,512]{1,0:T(8,128)(2,1)}, bf16[2,512,768]{2,1,...) custom-call(s32[1]{0:T(128)} %bitcast.me_ref.refs_0_, s32[16,8,896]{2,1,0:T(8,128)} %copy-done.10, ...), custom_call_target="tpu_custom_call" | custom-call | flops 33999998976 | bytes 1000000 | tf_op jit(solution)/shard_map/tables/pallas_call | solution.py:539
  68.9 3.8 %copy.17.refs_9_.refs_2_ = f32[16,16,2,768]{3,2,1,0:T(2,128)} copy(f32[16,16,2,768]{3,1,2,0:T(8,128)} %all-gather.2.cloned.1.call-done) | data formatting | bytes 3145728 | tf_op jit(solution)/shard_map/all_gather | solution.py:523
  72.7 7.8 %last_sums.3 = (f32[8,160,256]{2,1,0:T(8,128)}, f32[4,160,256]{2,1,0:T(8,128)}, f32[4,160,256]{2,1,0:T(8,128)}) custom-call(s32[1]{0:T(128)} %bitcast.me_ref.refs_0_, s32[1]{0:T(128)} %get-tuple-element.27.refs_1_, bf16[1536,768]{1,0:T(8,128)(2,1)} %refs_2_.7, s32[2,1536]{1,0:T(2,128)} %refs_3_.7, bf16[2048,512]{1,0:T(8,128)(2,1)} %get-tuple-element.28.refs_4_, ...), custom_call_target="tpu_custom_call" | custom-call | flops 8999999488 | bytes 1000000 | tf_op jit(solution)/shard_map/last_sums/pallas_call | solution.py:574
  80.6 7.9 %last_sums.5 = (f32[8,160,256]{2,1,0:T(8,128)}, f32[4,160,256]{2,1,0:T(8,128)}, f32[4,160,256]{2,1,0:T(8,128)}) custom-call(s32[1]{0:T(128)} %bitcast.me_ref.refs_0_, s32[1]{0:T(128)} %get-tuple-element.27.refs_1_, bf16[1536,768]{1,0:T(8,128)(2,1)} %refs_2_.7, s32[2,1536]{1,0:T(2,128)} %refs_3_.7, bf16[2048,512]{1,0:T(8,128)(2,1)} %get-tuple-element.28.refs_4_, ...), custom_call_target="tpu_custom_call" | custom-call | flops 8999999488 | bytes 1000000 | tf_op jit(solution)/shard_map/last_sums/pallas_call | solution.py:574
  89.0 1.0 slice_add_fusion
  90.0 8.2 %last_sums.4 = (f32[8,160,256]{2,1,0:T(8,128)}, f32[4,160,256]{2,1,0:T(8,128)}, f32[4,160,256]{2,1,0:T(8,128)}) custom-call(s32[1]{0:T(128)} %bitcast.me_ref.refs_0_, s32[1]{0:T(128)} %get-tuple-element.27.refs_1_, bf16[1536,768]{1,0:T(8,128)(2,1)} %refs_2_.7, s32[2,1536]{1,0:T(2,128)} %refs_3_.7, bf16[2048,512]{1,0:T(8,128)(2,1)} %get-tuple-element.28.refs_4_, ...), custom_call_target="tpu_custom_call" | custom-call | flops 8999999488 | bytes 1000000 | tf_op jit(solution)/shard_map/last_sums/pallas_call | solution.py:574
  99.1 0.8 collective-permute-start.11
  99.9 15.6 %collective-permute-done.14 = f32[4,160,256]{2,1,0:T(8,128)S(1)} collective-permute-done((f32[4,160,256]{2,1,0:T(8,128)S(1)}, f32[4,160,256]{2,1,0:T(8,128)S(1)}, u32[]{:S(2)}, u32[]{:S(2)}) %collective-permute-start.14) | collective-permute-done | bytes 655392 | tf_op jit(solution)/shard_map/ppermute | solution.py:454
  115.5 0.7 collective-permute-start.15
  117.2 3.6 %collective-permute-start.12 = (f32[2,160,256]{2,1,0:T(8,128)S(1)}, f32[2,160,256]{2,1,0:T(8,128)S(1)}, u32[]{:S(2)}, u32[]{:S(2)}) collective-permute-start(f32[2,160,256]{2,1,0:T(8,128)S(1)} %get-tuple-element.53), channel_id=1, source_target_pairs={{0,8},{1,9},{2,10},{3,11},{4,12},{5,13},{6,14},{7,15},{8,0},{9,1},... | collective-permute-start | bytes 983048 | tf_op jit(solution)/shard_map/ppermute | solution.py:454
  120.7 10.2 %collective-permute-done.15 = f32[2,160,256]{2,1,0:T(8,128)S(1)} collective-permute-done((f32[2,160,256]{2,1,0:T(8,128)S(1)}, f32[2,160,256]{2,1,0:T(8,128)S(1)}, u32[]{:S(2)}, u32[]{:S(2)}) %collective-permute-start.15) | collective-permute-done | bytes 327712 | tf_op jit(solution)/shard_map/ppermute | solution.py:454
  131.1 8.1 %collective-permute-done.12 = f32[2,160,256]{2,1,0:T(8,128)S(1)} collective-permute-done((f32[2,160,256]{2,1,0:T(8,128)S(1)}, f32[2,160,256]{2,1,0:T(8,128)S(1)}, u32[]{:S(2)}, u32[]{:S(2)}) %collective-permute-start.12) | collective-permute-done | bytes 327712 | tf_op jit(solution)/shard_map/ppermute | solution.py:454
  139.1 2.4 %collective-permute-start.13 = (f32[1,160,256]{2,1,0:T(8,128)S(1)}, f32[1,160,256]{2,1,0:T(8,128)S(1)}, u32[]{:S(2)}, u32[]{:S(2)}) collective-permute-start(f32[1,160,256]{2,1,0:T(8,128)S(1)} %slice_add_fusion.14), channel_id=1, source_target_pairs={{0,2},{1,3},{2,0},{3,1},{4,6},{5,7},{6,4},{7,5},{8,10},{9,11},{10,... | collective-permute-start | bytes 491528 | tf_op jit(solution)/shard_map/ppermute | solution.py:454
  141.9 0.7 fusion.1.refs_3_
  142.6 2.2 %collective-permute-done.13 = f32[1,160,256]{2,1,0:T(8,128)S(1)} collective-permute-done((f32[1,160,256]{2,1,0:T(8,128)S(1)}, f32[1,160,256]{2,1,0:T(8,128)S(1)}, u32[]{:S(2)}, u32[]{:S(2)}) %collective-permute-start.13) | collective-permute-done | bytes 163872 | tf_op jit(solution)/shard_map/ppermute | solution.py:454
  144.8 0.7 fusion.3.refs_3_
  145.5 3.3 %collective-permute-done.8 = f32[2,160,256]{2,1,0:T(8,128)S(1)} collective-permute-done((f32[2,160,256]{2,1,0:T(8,128)S(1)}, f32[2,160,256]{2,1,0:T(8,128)S(1)}, u32[]{:S(2)}, u32[]{:S(2)}) %collective-permute-start.8) | collective-permute-done | bytes 327712 | tf_op jit(solution)/shard_map/ppermute | solution.py:454
  148.8 1.1 collective-permute-start.9
  149.9 2.5 %outputs.3 = (f32[512,768]{1,0:T(8,128)}, f32[128,768]{1,0:T(8,128)}) custom-call(s32[1]{0:T(128)} %bitcast.me_ref.refs_0_, f32[512,768]{1,0:T(8,128)} %refs_0_.11, f32[2048,768]{1,0:T(8,128)} %refs_1_.11, f32[16,16,2,768]{3,2,1,0:T(2,128)} %copy.17.refs_9_.refs_2_, f32[160,256]{1,0:T(8,128)} %fusion.1.refs_3_, f32[2048,128]{1,0:T(8,128)} %get-tuple-element.38.refs_4_, ...), custom_call_target="tpu_custom_call" | custom-call | flops 1000000000 | bytes 1000000 | tf_op jit(solution)/shard_map/outputs/pallas_call | solution.py:604
  152.4 2.5 %outputs.4 = (f32[512,768]{1,0:T(8,128)}, f32[128,768]{1,0:T(8,128)}) custom-call(s32[1]{0:T(128)} %bitcast.me_ref.refs_0_, f32[512,768]{1,0:T(8,128)} %refs_0_.11, f32[2048,768]{1,0:T(8,128)} %refs_1_.11, f32[16,16,2,768]{3,2,1,0:T(2,128)} %copy.17.refs_9_.refs_2_, f32[160,256]{1,0:T(8,128)} %fusion.3.refs_3_, ...), custom_call_target="tpu_custom_call", output_to_operand_aliasing={{0}: (7, {}), {1}: (8, {})} | custom-call | flops 1000000000 | bytes 1000000 | tf_op jit(solution)/shard_map/outputs/pallas_call | solution.py:604
  154.9 1.4 collective-permute-done.9
  157.0 2.5 %outputs.5 = (f32[512,768]{1,0:T(8,128)}, f32[128,768]{1,0:T(8,128)}) custom-call(s32[1]{0:T(128)} %bitcast.me_ref.refs_0_, f32[512,768]{1,0:T(8,128)} %refs_0_.11, f32[2048,768]{1,0:T(8,128)} %refs_1_.11, f32[16,16,2,768]{3,2,1,0:T(2,128)} %copy.17.refs_9_.refs_2_, f32[160,256]{1,0:T(8,128)} %fusion.5.refs_3_, ...), custom_call_target="tpu_custom_call", output_to_operand_aliasing={{0}: (7, {}), {1}: (8, {})} | custom-call | flops 1000000000 | bytes 1000000 | tf_op jit(solution)/shard_map/outputs/pallas_call | solution.py:604
  (62 shorter events, 5.8 us)
Async XLA Ops:
  7.2 61.7 %all-gather.2.cloned.1.call-start = ((), (), s32[]{:S(2)}) async-start(), calls=%async_computation | async-start | bytes 1671168 | tf_op jit(solution)/shard_map/all_gather | solution.py:523
  9.4 13.9 %collective-permute-start = (s32[8,896]{1,0:T(8,128)S(1)}, s32[8,896]{1,0:T(8,128)S(1)}, u32[]{:S(2)}, u32[]{:S(2)}) collective-permute-start(s32[8,896]{1,0:T(8,128)S(1)} %get-tuple-element.71), channel_id=1, source_target_pairs={{0,4},{1,5},{2,6},{3,7},{4,0},{5,1},{6,2},{7,3},{8,12},{9,13},{10,... | collective-permute-start | bytes 86024 | tf_op jit(solution)/shard_map/ppermute | solution.py:454
  12.4 10.8 %collective-permute-start.1 = (s32[8,896]{1,0:T(8,128)S(1)}, s32[8,896]{1,0:T(8,128)S(1)}, u32[]{:S(2)}, u32[]{:S(2)}) collective-permute-start(s32[8,896]{1,0:T(8,128)S(1)} %get-tuple-element.71), channel_id=1, source_target_pairs={{0,8},{1,9},{2,10},{3,11},{4,12},{5,13},{6,14},{7,15},{8,0},{9,1},... | collective-permute-start | bytes 86024 | tf_op jit(solution)/shard_map/ppermute | solution.py:454
  15.0 8.2 %collective-permute-start.2 = (s32[8,896]{1,0:T(8,128)S(1)}, s32[8,896]{1,0:T(8,128)S(1)}, u32[]{:S(2)}, u32[]{:S(2)}) collective-permute-start(s32[8,896]{1,0:T(8,128)S(1)} %get-tuple-element.71), channel_id=1, source_target_pairs={{0,12},{1,13},{2,14},{3,15},{4,8},{5,9},{6,10},{7,11},{8,4},{9,5},... | collective-permute-start | bytes 86024 | tf_op jit(solution)/shard_map/ppermute | solution.py:454
  15.0 8.2 %copy-start.8 = (s32[2,32]{1,0:T(2,128)S(1)}, s32[2,32]{1,0:T(2,128)}, u32[]{:S(2)}) copy-start(s32[2,32]{1,0:T(2,128)} %param.9) | copy-start | bytes 772
  23.3 1.8 %copy-start.7 = (s32[4,8,896]{2,1,0:T(8,128)}, s32[4,8,896]{2,1,0:T(8,128)S(1)}, u32[]{:S(2)}) copy-start(s32[4,8,896]{2,1,0:T(8,128)S(1)} %pad_add_fusion.refs_2_) | copy-start | bytes 344068
  23.3 7.8 %collective-permute-start.3 = (s32[4,8,896]{2,1,0:T(8,128)S(1)}, s32[4,8,896]{2,1,0:T(8,128)S(1)}, u32[]{:S(2)}, u32[]{:S(2)}) collective-permute-start(s32[4,8,896]{2,1,0:T(8,128)S(1)} %pad_add_fusion.refs_2_), channel_id=1, source_target_pairs={{0,2},{1,3},{2,0},{3,1},{4,6},{5,7},{6,4},{7,5},{8,10},{9,11},{10,... | collective-permute-start | bytes 344072 | tf_op jit(solution)/shard_map/ppermute | solution.py:454
  31.2 0.7 copy-start.9
  31.2 6.7 %collective-permute-start.4 = (s32[8,8,896]{2,1,0:T(8,128)S(1)}, s32[8,8,896]{2,1,0:T(8,128)S(1)}, u32[]{:S(2)}, u32[]{:S(2)}) collective-permute-start(s32[8,8,896]{2,1,0:T(8,128)S(1)} %get-tuple-element.60.refs_2_), channel_id=1, source_target_pairs={{0,1},{1,0},{2,3},{3,2},{4,5},{5,4},{6,7},{7,6},{8,9},{9,8},{10,11... | collective-permute-start | bytes 688136 | tf_op jit(solution)/shard_map/ppermute | solution.py:454
  37.9 0.8 copy-start.10
  80.5 8.5 %copy-start.5 = (f32[4,160,256]{2,1,0:T(8,128)S(1)}, f32[4,160,256]{2,1,0:T(8,128)}, u32[]{:S(2)}) copy-start(f32[4,160,256]{2,1,0:T(8,128)} %get-tuple-element.33) | copy-start | bytes 1966084
  80.5 8.5 %copy-start.6 = (f32[4,160,256]{2,1,0:T(8,128)S(1)}, f32[4,160,256]{2,1,0:T(8,128)}, u32[]{:S(2)}) copy-start(f32[4,160,256]{2,1,0:T(8,128)} %get-tuple-element.43) | copy-start | bytes 1966084
  80.5 8.5 %collective-permute-start.5 = (f32[8,160,256]{2,1,0:T(8,128)}, f32[8,160,256]{2,1,0:T(8,128)S(1)}, u32[]{:S(2)}, u32[]{:S(2)}) collective-permute-start(f32[8,160,256]{2,1,0:T(8,128)} %get-tuple-element.34), channel_id=1, source_target_pairs={{0,1},{1,0},{2,3},{3,2},{4,5},{5,4},{6,7},{7,6},{8,9},{9,8},{10,11... | collective-permute-start | bytes 3932168 | tf_op jit(solution)/shard_map/ppermute | solution.py:454
  88.5 10.4 %collective-permute-start.10 = (f32[8,160,256]{2,1,0:T(8,128)}, f32[8,160,256]{2,1,0:T(8,128)S(1)}, u32[]{:S(2)}, u32[]{:S(2)}) collective-permute-start(f32[8,160,256]{2,1,0:T(8,128)} %get-tuple-element.41), channel_id=1, source_target_pairs={{0,1},{1,0},{2,3},{3,2},{4,5},{5,4},{6,7},{7,6},{8,9},{9,8},{10,11... | collective-permute-start | bytes 3932168 | tf_op jit(solution)/shard_map/ppermute | solution.py:454
  90.0 8.3 %copy-start.4 = (f32[4,160,256]{2,1,0:T(8,128)S(1)}, f32[4,160,256]{2,1,0:T(8,128)}, u32[]{:S(2)}) copy-start(f32[4,160,256]{2,1,0:T(8,128)} %get-tuple-element.51.refs_9_) | copy-start | bytes 1966084
  90.0 8.9 %copy-start.2 = (f32[4,160,256]{2,1,0:T(8,128)S(1)}, f32[4,160,256]{2,1,0:T(8,128)}, u32[]{:S(2)}) copy-start(f32[4,160,256]{2,1,0:T(8,128)} %get-tuple-element.42) | copy-start | bytes 1966084
  90.0 8.9 %copy-start.3 = (f32[4,160,256]{2,1,0:T(8,128)S(1)}, f32[4,160,256]{2,1,0:T(8,128)}, u32[]{:S(2)}) copy-start(f32[4,160,256]{2,1,0:T(8,128)} %get-tuple-element.40) | copy-start | bytes 1966084
  98.2 18.1 %collective-permute-start.6 = (f32[8,160,256]{2,1,0:T(8,128)}, f32[8,160,256]{2,1,0:T(8,128)S(1)}, u32[]{:S(2)}, u32[]{:S(2)}) collective-permute-start(f32[8,160,256]{2,1,0:T(8,128)} %get-tuple-element.36), channel_id=1, source_target_pairs={{0,1},{1,0},{2,3},{3,2},{4,5},{5,4},{6,7},{7,6},{8,9},{9,8},{10,11... | collective-permute-start | bytes 3932168 | tf_op jit(solution)/shard_map/ppermute | solution.py:454
  98.4 17.1 %collective-permute-start.14 = (f32[4,160,256]{2,1,0:T(8,128)S(1)}, f32[4,160,256]{2,1,0:T(8,128)S(1)}, u32[]{:S(2)}, u32[]{:S(2)}) collective-permute-start(f32[4,160,256]{2,1,0:T(8,128)S(1)} %copy-done.4), channel_id=1, source_target_pairs={{0,2},{1,3},{2,0},{3,1},{4,6},{5,7},{6,4},{7,5},{8,10},{9,11},{10,... | collective-permute-start | bytes 1966088 | tf_op jit(solution)/shard_map/ppermute | solution.py:454
  99.1 17.2 %copy-start = (f32[4,160,256]{2,1,0:T(8,128)S(1)}, f32[4,160,256]{2,1,0:T(8,128)}, u32[]{:S(2)}) copy-start(f32[4,160,256]{2,1,0:T(8,128)} %get-tuple-element.37) | copy-start | bytes 1966084
  99.1 17.2 %copy-start.1 = (f32[4,160,256]{2,1,0:T(8,128)S(1)}, f32[4,160,256]{2,1,0:T(8,128)}, u32[]{:S(2)}) copy-start(f32[4,160,256]{2,1,0:T(8,128)} %get-tuple-element.35) | copy-start | bytes 1966084
  99.1 18.0 %collective-permute-start.11 = (f32[4,160,256]{2,1,0:T(8,128)S(1)}, f32[4,160,256]{2,1,0:T(8,128)S(1)}, u32[]{:S(2)}, u32[]{:S(2)}) collective-permute-start(f32[4,160,256]{2,1,0:T(8,128)S(1)} %get-tuple-element.55), channel_id=1, source_target_pairs={{0,4},{1,5},{2,6},{3,7},{4,0},{5,1},{6,2},{7,3},{8,12},{9,13},{10,... | collective-permute-start | bytes 1966088 | tf_op jit(solution)/shard_map/ppermute | solution.py:454
  115.5 15.4 %collective-permute-start.15 = (f32[2,160,256]{2,1,0:T(8,128)S(1)}, f32[2,160,256]{2,1,0:T(8,128)S(1)}, u32[]{:S(2)}, u32[]{:S(2)}) collective-permute-start(f32[2,160,256]{2,1,0:T(8,128)S(1)} %get-tuple-element.49), channel_id=1, source_target_pairs={{0,4},{1,5},{2,6},{3,7},{4,0},{5,1},{6,2},{7,3},{8,12},{9,13},{10,... | collective-permute-start | bytes 983048 | tf_op jit(solution)/shard_map/ppermute | solution.py:454
  116.5 25.0 %collective-permute-start.7 = (f32[4,160,256]{2,1,0:T(8,128)S(1)}, f32[4,160,256]{2,1,0:T(8,128)S(1)}, u32[]{:S(2)}, u32[]{:S(2)}) collective-permute-start(f32[4,160,256]{2,1,0:T(8,128)S(1)} %get-tuple-element.59), channel_id=1, source_target_pairs={{0,2},{1,3},{2,0},{3,1},{4,6},{5,7},{6,4},{7,5},{8,10},{9,11},{10,... | collective-permute-start | bytes 1966088 | tf_op jit(solution)/shard_map/ppermute | solution.py:454
  117.2 21.9 %collective-permute-start.12 = (f32[2,160,256]{2,1,0:T(8,128)S(1)}, f32[2,160,256]{2,1,0:T(8,128)S(1)}, u32[]{:S(2)}, u32[]{:S(2)}) collective-permute-start(f32[2,160,256]{2,1,0:T(8,128)S(1)} %get-tuple-element.53), channel_id=1, source_target_pairs={{0,8},{1,9},{2,10},{3,11},{4,12},{5,13},{6,14},{7,15},{8,0},{9,1},... | collective-permute-start | bytes 983048 | tf_op jit(solution)/shard_map/ppermute | solution.py:454
  131.0 10.9 %collective-permute-start.16 = (f32[1,160,256]{2,1,0:T(8,128)S(1)}, f32[1,160,256]{2,1,0:T(8,128)S(1)}, u32[]{:S(2)}, u32[]{:S(2)}) collective-permute-start(f32[1,160,256]{2,1,0:T(8,128)S(1)} %slice_add_fusion.12), channel_id=1, source_target_pairs={{0,8},{1,9},{2,10},{3,11},{4,12},{5,13},{6,14},{7,15},{8,0},{9,1},... | collective-permute-start | bytes 491528 | tf_op jit(solution)/shard_map/ppermute | solution.py:454
  139.1 5.7 %collective-permute-start.13 = (f32[1,160,256]{2,1,0:T(8,128)S(1)}, f32[1,160,256]{2,1,0:T(8,128)S(1)}, u32[]{:S(2)}, u32[]{:S(2)}) collective-permute-start(f32[1,160,256]{2,1,0:T(8,128)S(1)} %slice_add_fusion.14), channel_id=1, source_target_pairs={{0,2},{1,3},{2,0},{3,1},{4,6},{5,7},{6,4},{7,5},{8,10},{9,11},{10,... | collective-permute-start | bytes 491528 | tf_op jit(solution)/shard_map/ppermute | solution.py:454
  141.6 7.2 %collective-permute-start.8 = (f32[2,160,256]{2,1,0:T(8,128)S(1)}, f32[2,160,256]{2,1,0:T(8,128)S(1)}, u32[]{:S(2)}, u32[]{:S(2)}) collective-permute-start(f32[2,160,256]{2,1,0:T(8,128)S(1)} %get-tuple-element.57), channel_id=1, source_target_pairs={{0,4},{1,5},{2,6},{3,7},{4,0},{5,1},{6,2},{7,3},{8,12},{9,13},{10,... | collective-permute-start | bytes 983048 | tf_op jit(solution)/shard_map/ppermute | solution.py:454
  148.8 7.5 %collective-permute-start.9 = (f32[1,160,256]{2,1,0:T(8,128)S(1)}, f32[1,160,256]{2,1,0:T(8,128)S(1)}, u32[]{:S(2)}, u32[]{:S(2)}) collective-permute-start(f32[1,160,256]{2,1,0:T(8,128)S(1)} %slice_add_fusion.16), channel_id=1, source_target_pairs={{0,8},{1,9},{2,10},{3,11},{4,12},{5,13},{6,14},{7,15},{8,0},{9,1},... | collective-permute-start | bytes 491528 | tf_op jit(solution)/shard_map/ppermute | solution.py:454
Sparse Core Ops, SparseCore 0:
  23.3 41.1 all-gather.1
